TPU v7x, 256 devices: a whole 4x4x8 slice. The times are simulated.
256 devices in a mesh: storey: 64 (over z, y, core), inner: 4 (over x).
Axes of the slice: x: 4, y: 4, z: 8, core: 2. Of those that a mesh axis runs over, the one named last changes fastest.
Arguments:
- synthesis: bfloat16 [3072, 3072], P('inner'), may hold values from -0.109375 to 0.109375
- analysis: bfloat16 [3072, 3072], P(None, 'inner'), may hold values from -0.109375 to 0.109375
- pivot: float32 [128, 3072], P('storey', 'inner'), may hold values from 0.1 to 0.4
- transfer: float32 [128, 3072], P('storey', 'inner'), may hold values from -1 to 1, as said below
- displacement: float32 [128, 3072], P('storey', 'inner'), may hold values from -6 to 6
- directions: bfloat16 [3072, 128, 128], P('inner', 'storey'), may hold values from -6 to 6
- sensor_pairs: int32 [128, 512, 2], P('storey'), may hold values from 0 to 3071
- sensor_weights: float32 [128, 512], P('storey'), may hold values from 0.1 to 1
Outputs:
- curvature_product: float32 [3072, 128, 128], P('inner', 'storey')
Inputs may be any that keep to these rules, and one draw needn't show every extreme that they name: `sensor_pairs`: each sensor's two degree-of-freedom indices within its storey's interface. `transfer`: magnitudes below one.
All inputs are finite; a program needn't handle non-finite values.
Results may differ from a plain program's by a relative error of at most 0.017.
Values may be sent and summed in bfloat16 or wider, within the bound.
A program may use at most 128 MiB of HBM per device.

v0:
```python
import jax
import jax.numpy as jnp
from jax import lax
from jax.sharding import PartitionSpec as P


def prefix(part, axis, combine, identity, reverse):
    count = lax.axis_size(axis)
    place = lax.axis_index(axis)
    ahead = count - 1 - place if reverse else place
    gathered = jax.tree.map(lambda a: lax.all_gather(a, axis), part)
    state = jax.tree.map(lambda a, e: jnp.zeros_like(a) + jnp.asarray(e, a.dtype), part, identity)

    def one(hop, state):
        source = count - 1 - hop if reverse else hop
        return combine(
            state, jax.tree.map(lambda a: lax.dynamic_index_in_dim(a, source, 0, False), gathered)
        )

    return lax.fori_loop(0, ahead, one, state)


def affine(earlier, following):
    rate_early, shift_early = earlier
    rate_late, shift_late = following
    return (rate_late * rate_early, rate_late[..., None] * shift_early + shift_late)


def sweep_chain(rate_rows, shifts, incoming_rule):
    cum_rate, cum_shift = lax.associative_scan(affine, (rate_rows, shifts), axis=1)
    incoming = incoming_rule((cum_rate[:, -1], cum_shift[:, -1]))
    states = cum_rate[:, :, None] * incoming[:, None, :] + cum_shift
    return (states, incoming)


def descend_chain(rate_rows, sources, incoming_rule):
    flipped_rate = rate_rows[:, ::-1]
    flipped_source = sources[:, ::-1]
    carried, incoming = sweep_chain(
        flipped_rate, flipped_rate[:, :, None] * flipped_source, incoming_rule
    )
    previous = jnp.concatenate([incoming[:, None, :], carried[:, :-1]], axis=1)
    return (flipped_source + previous)[:, ::-1]


def climb_in(summary):
    identity = (jnp.ones_like(summary[0]), jnp.zeros_like(summary[1]))
    return prefix(summary, "storey", affine, identity, False)[1]


def descend_in(summary):
    identity = (jnp.ones_like(summary[0]), jnp.zeros_like(summary[1]))
    return prefix(summary, "storey", affine, identity, True)[1]


def split_parts(values):
    upper_portion = values.astype(jnp.bfloat16)
    rest_part = (values - upper_portion.astype(jnp.float32)).astype(jnp.bfloat16)
    return (upper_portion, rest_part)


def local(
    synthesis, analysis, pivot, transfer, displacement, directions, sensor_pairs, sensor_weights
):
    motion_variable_entries, storey_rows, columns = directions.shape
    flat_cols = storey_rows * columns
    load_scale = displacement.T[:, :, None]
    tangent_load = (
        (-(load_scale * directions.astype(jnp.float32)))
        .astype(jnp.bfloat16)
        .reshape(motion_variable_entries, flat_cols)
    )
    rows_part = analysis
    modal_load = lax.psum_scatter(
        jnp.dot(rows_part, tangent_load, preferred_element_type=jnp.float32),
        "inner",
        scatter_dimension=0,
        tiled=True,
    ).reshape(motion_variable_entries, storey_rows, columns)
    pivot_local = pivot.T
    transfer_local = transfer.T
    climbed, unused = sweep_chain(transfer_local, pivot_local[:, :, None] * modal_load, climb_in)
    modal_round = climbed.astype(jnp.bfloat16)
    cols_part = synthesis
    tangent = jnp.dot(
        cols_part,
        lax.all_gather(
            modal_round.reshape(motion_variable_entries, flat_cols), "inner", axis=0, tiled=True
        ),
        preferred_element_type=jnp.float32,
    )
    tangent = tangent.reshape(motion_variable_entries, storey_rows, columns)
    first_dof = lax.axis_index("inner") * motion_variable_entries
    dof_ids = first_dof + jnp.arange(motion_variable_entries, dtype=jnp.int32)
    upper_dof = sensor_pairs[:, :, 0]
    lower_dof = sensor_pairs[:, :, 1]
    incidence = (
        (upper_dof[:, :, None] == dof_ids).astype(jnp.float32)
        - (lower_dof[:, :, None] == dof_ids).astype(jnp.float32)
    ).astype(jnp.bfloat16)
    directional_derivative_top, tangent_rest = split_parts(tangent)
    partial_read = jnp.einsum(
        "kmr,rkc->kmc", incidence, directional_derivative_top, preferred_element_type=jnp.float32
    )
    partial_read = partial_read + jnp.einsum(
        "kmr,rkc->kmc", incidence, tangent_rest, preferred_element_type=jnp.float32
    )
    readings = lax.psum(partial_read.astype(jnp.bfloat16), "inner").astype(jnp.float32)
    weighted = sensor_weights[:, :, None] * readings
    weighted_high, weighted_rest = split_parts(weighted)
    adjoint_load = jnp.einsum(
        "kmr,kmc->rkc", incidence, weighted_high, preferred_element_type=jnp.float32
    )
    adjoint_load = adjoint_load + jnp.einsum(
        "kmr,kmc->rkc", incidence, weighted_rest, preferred_element_type=jnp.float32
    )
    adjoint_load = adjoint_load.astype(jnp.bfloat16).reshape(motion_variable_entries, flat_cols)
    cols_part = synthesis
    modal_adjoint = (
        lax.psum_scatter(
            lax.dot_general(
                cols_part,
                adjoint_load,
                (((0,), (0,)), ((), ())),
                preferred_element_type=jnp.float32,
            ).astype(jnp.bfloat16),
            "inner",
            scatter_dimension=0,
            tiled=True,
        )
        .astype(jnp.float32)
        .reshape(motion_variable_entries, storey_rows, columns)
    )
    gathered_sum = descend_chain(transfer_local, modal_adjoint, descend_in)
    weighted_modes = (pivot_local[:, :, None] * gathered_sum).astype(jnp.bfloat16)
    rows_part = analysis
    response = lax.dot_general(
        rows_part,
        lax.all_gather(
            weighted_modes.reshape(motion_variable_entries, flat_cols), "inner", axis=0, tiled=True
        ),
        (((0,), (0,)), ((), ())),
        preferred_element_type=jnp.float32,
    )
    response = response.reshape(motion_variable_entries, storey_rows, columns)
    return -load_scale * response


def solution(mesh):
    return jax.shard_map(
        local,
        mesh=mesh,
        in_specs=(
            P("inner", None),
            P(None, "inner"),
            P("storey", "inner"),
            P("storey", "inner"),
            P("storey", "inner"),
            P("inner", "storey", None),
            P("storey", None, None),
            P("storey", None),
        ),
        out_specs=P("inner", "storey", None),
        check_vma=False,
    )
```

profile of v0, /device:TPU:1, one launch (start us, length us, event | category | flops | bytes accessed | tf_op | source)
XLA Modules:
  0.0 666.5 jit_solution(9600807979473085333)
XLA Ops:
  7.4 1.9 negate_convert_fusion
  9.3 5.4 convolution_bitcast_fusion
  15.5 44.1 %reduce-scatter.3.cloned.1.call-done = f32[768,256]{0,1:T(8,128)} async-done(((f32[3072,256]{0,1:T(8,128)}), f32[768,256]{0,1:T(8,128)}) %reduce-scatter.3.cloned.1.call-update) | async-done | bytes 786448 | tf_op jit(solution)/shard_map/reduce_scatter | solution.py:74
  59.6 1.2 broadcast_multiply_fusion
  61.7 45.4 %all-gather = f32[49152,1]{0,1:T(1,128)S(1)} all-gather(f32[768,1]{0,1:T(1,128)S(1)} %get-tuple-element.181), channel_id=2, replica_groups=mesh['storey'=64,'inner'=4] {'storey'}, dimensions={0}, use_global_device_ids=true | all-gather | bytes 199680 | tf_op jit(solution)/shard_map/all_gather | solution.py:11
  108.7 75.0 %all-gather.13.cloned.1.call-done = f32[49152,1,128]{0,2,1:T(8,128)} async-done(((f32[768,1,128]{0,2,1:T(8,128)}), f32[49152,1,128]{0,2,1:T(8,128)}) %all-gather.13.cloned.1.call-update) | async-done | bytes 25165840 | tf_op jit(solution)/shard_map/all_gather | solution.py:11
  183.7 24.6 %copy.32 = f32[49152,1,128]{2,0,1:T(8,128)} copy(f32[49152,1,128]{0,2,1:T(8,128)} %all-gather.13.cloned.1.call-done) | data formatting | bytes 50331648 | tf_op jit(solution)/shard_map/while | solution.py:20
  208.4 1.2 while.26
  208.5 1.2 bitcast_add_fusion.4
  210.8 100.2 %all-gather.9.cloned.1.call-done = bf16[3072,256]{0,1:T(8,128)(2,1)} async-done(((bf16[768,256]{0,1:T(8,128)(2,1)}), bf16[3072,256]{0,1:T(8,128)(2,1)}) %all-gather.9.cloned.1.call-update) | async-done | bytes 1572880 | tf_op jit(solution)/shard_map/all_gather | solution.py:87
  311.0 4.2 fusion.40
  316.3 1.7 fusion.20
  318.1 44.8 %all-reduce.9.cloned.1.call-done = bf16[2,512,128]{2,1,0:T(8,128)(2,1)} async-done(((bf16[2,512,128]{2,1,0:T(8,128)(2,1)}), bf16[2,512,128]{2,1,0:T(8,128)(2,1)}) %all-reduce.9.cloned.1.call-update) | async-done | bytes 262160 | tf_op jit(solution)/shard_map/psum | solution.py:108
  362.9 2.2 fusion.1
  365.1 1.2 fusion.18
  366.3 4.9 fusion
  371.5 29.7 %reduce-scatter.5.cloned.1.call-done = bf16[768,256]{0,1:T(8,128)(2,1)} async-done(((bf16[3072,256]{0,1:T(8,128)(2,1)}), bf16[768,256]{0,1:T(8,128)(2,1)}) %reduce-scatter.5.cloned.1.call-update) | async-done | bytes 393232 | tf_op jit(solution)/shard_map/reduce_scatter | solution.py:120
  403.3 46.7 %all-gather.2 = f32[49152,1]{0,1:T(1,128)S(1)} all-gather(f32[768,1]{0,1:T(1,128)S(1)} %get-tuple-element.180), channel_id=4, replica_groups=mesh['storey'=64,'inner'=4] {'storey'}, dimensions={0}, use_global_device_ids=true | all-gather | bytes 199680 | tf_op jit(solution)/shard_map/all_gather | solution.py:11
  451.0 75.7 %all-gather.15.cloned.1.call-done = f32[49152,1,128]{0,2,1:T(8,128)} async-done(((f32[768,1,128]{0,2,1:T(8,128)}), f32[49152,1,128]{0,2,1:T(8,128)}) %all-gather.15.cloned.1.call-update) | async-done | bytes 25165840 | tf_op jit(solution)/shard_map/all_gather | solution.py:11
  526.8 24.6 %copy.33 = f32[49152,1,128]{2,0,1:T(8,128)} copy(f32[49152,1,128]{0,2,1:T(8,128)} %all-gather.15.cloned.1.call-done) | data formatting | bytes 50331648 | tf_op jit(solution)/shard_map/while | solution.py:20
  551.4 76.9 %while.27 = (s32[]{:T(128)}, f32[768,128]{1,0:T(8,128)S(1)}, s32[]{:T(128)}, f32[64,768]{1,0:T(8,128)S(1)}, f32[64,768,128]{2,1,0:T(8,128)}, /*index=5*/s32[]{:T(128)}, s32[]{:T(128)}, s32[]{:T(128)}, s32[]{:T(128)}) while((s32[]{:T(128)}, f32[768,128]{1,0:T(8,128)S(1)}, s32[]{:T(128)}, f32[64,768]{1,0:T(8,128)S(1)}, ...), condition=%wide.region_6.7_spmd, body=%wide.region_5.6_spmd.sunk | while | flops 196614 | bytes 1189011 | solution.py:20
  551.5 1.2 bitcast_add_fusion.5
  552.7 1.2 bitcast_add_fusion.5
  554.0 1.2 bitcast_add_fusion.5
  555.2 1.2 bitcast_add_fusion.5
  556.4 1.2 bitcast_add_fusion.5
  557.7 1.2 bitcast_add_fusion.5
  558.9 1.2 bitcast_add_fusion.5
  560.2 1.2 bitcast_add_fusion.5
  561.4 1.2 bitcast_add_fusion.5
  562.6 1.2 bitcast_add_fusion.5
  563.9 1.2 bitcast_add_fusion.5
  565.1 1.2 bitcast_add_fusion.5
  566.4 1.2 bitcast_add_fusion.5
  567.6 1.2 bitcast_add_fusion.5
  568.9 1.2 bitcast_add_fusion.5
  570.1 1.2 bitcast_add_fusion.5
  571.3 1.2 bitcast_add_fusion.5
  572.6 1.2 bitcast_add_fusion.5
  573.8 1.2 bitcast_add_fusion.5
  575.1 1.2 bitcast_add_fusion.5
  576.3 1.2 bitcast_add_fusion.5
  577.5 1.2 bitcast_add_fusion.5
  578.8 1.2 bitcast_add_fusion.5
  580.0 1.2 bitcast_add_fusion.5
  581.3 1.2 bitcast_add_fusion.5
  582.5 1.2 bitcast_add_fusion.5
  583.7 1.2 bitcast_add_fusion.5
  585.0 1.2 bitcast_add_fusion.5
  586.2 1.2 bitcast_add_fusion.5
  587.5 1.2 bitcast_add_fusion.5
  588.7 1.2 bitcast_add_fusion.5
  592.4 1.2 bitcast_add_fusion.5
  596.1 1.2 bitcast_add_fusion.5
  601.1 1.2 bitcast_add_fusion.5
  604.8 1.2 bitcast_add_fusion.5
  608.5 1.2 bitcast_add_fusion.5
  612.3 1.2 bitcast_add_fusion.5
  616.0 1.2 bitcast_add_fusion.5
  619.7 1.2 bitcast_add_fusion.5
  624.7 1.2 bitcast_add_fusion.5
  629.7 23.5 %all-gather.11.cloned.1.call-done = bf16[3072,256]{0,1:T(8,128)(2,1)} async-done(((bf16[768,256]{0,1:T(8,128)(2,1)}), bf16[3072,256]{0,1:T(8,128)(2,1)}) %all-gather.11.cloned.1.call-update) | async-done | bytes 1572880 | tf_op jit(solution)/shard_map/all_gather | solution.py:139
  653.2 4.2 fusion.41
  657.9 1.7 broadcast_multiply_fusion.1
  (144 shorter events, 38.6 us)
Async XLA Ops:
  6.5 53.0 %reduce-scatter.3.cloned.1.call-start = ((), (), s32[]{:S(2)}) async-start(), calls=%async_computation.2 | async-start | bytes 3932160 | tf_op jit(solution)/shard_map/reduce_scatter | solution.py:74
  14.8 0.7 copy-start.1
  14.8 44.8 %copy-start = (f32[2,768]{1,0:T(2,128)S(1)}, f32[2,768]{1,0:T(2,128)}, u32[]{:S(2)}) copy-start(f32[2,768]{1,0:T(2,128)} %param.14) | copy-start | bytes 18436
  14.8 168.9 %all-gather.13.cloned.1.call-start = ((), (), s32[]{:S(2)}) async-start(), calls=%async_computation.7 | async-start | bytes 25559040 | tf_op jit(solution)/shard_map/all_gather | solution.py:11
  61.6 249.4 %all-gather.9.cloned.1.call-start = ((), (), s32[]{:S(2)}) async-start(), calls=%async_computation.3 | async-start | bytes 1966080 | tf_op jit(solution)/shard_map/all_gather | solution.py:87
  208.4 2.4 copy-start.3
  210.7 152.2 %all-reduce.9.cloned.1.call-start = ((), (), s32[]{:S(2)}) async-start(), calls=%async_computation.4 | async-start | bytes 524288 | tf_op jit(solution)/shard_map/psum | solution.py:108
  315.5 47.4 %copy-start.5 = (f32[2,512]{1,0:T(2,128)S(1)}, f32[2,512]{1,0:T(2,128)}, u32[]{:S(2)}) copy-start(f32[2,512]{1,0:T(2,128)} %param.19) | copy-start | bytes 12292
  318.0 83.2 %reduce-scatter.5.cloned.1.call-start = ((), (), s32[]{:S(2)}) async-start(), calls=%async_computation.5 | async-start | bytes 1966080 | tf_op jit(solution)/shard_map/reduce_scatter | solution.py:120
  362.9 2.2 copy-start.4
  371.3 155.5 %all-gather.15.cloned.1.call-start = ((), (), s32[]{:S(2)}) async-start(), calls=%async_computation.8 | async-start | bytes 25559040 | tf_op jit(solution)/shard_map/all_gather | solution.py:11
  403.2 250.0 %all-gather.11.cloned.1.call-start = ((), (), s32[]{:S(2)}) async-start(), calls=%async_computation.6 | async-start | bytes 1966080 | tf_op jit(solution)/shard_map/all_gather | solution.py:139
  628.4 1.2 copy-start.2
Sparse Core Ops, SparseCore 0:
  14.9 44.6 reduce-scatter.2
  62.3 121.4 all-gather.12
  210.8 100.1 all-gather.8
  318.1 44.7 all-reduce.8
  371.4 29.8 reduce-scatter.4
  404.1 122.5 all-gather.14
  629.6 23.5 all-gather.10
where the time goes:
time: 670 us; the launch traced here: 666 us
  waiting for transfers between devices  393 us (59%)
  blocking collectives  92.1 us (14%)
  other arithmetic  85.8 us (13%)
  local copies, waits for them, and re-layouts  54.2 us (8%)
  matrix products  24.6 us (4%)
  between operations  13.8 us (2%)
    all_gather x2, waiting for transfers between devices, prefix(): gathered = jax.tree.map(lambda a: lax.all_gather(a, axis), part)  151 us
    all_gather x1, waiting for transfers between devices, local(): lax.all_gather(modal_round.reshape(motion_variable_entries, flat_cols), '...  100 us
    all_gather x2, blocking collectives, prefix(): gathered = jax.tree.map(lambda a: lax.all_gather(a, axis), part)  92.1 us
    add x63, other arithmetic, affine(): rate_late[..., None] * shift_early + shift_late  74.4 us
    while x4, local copies, waits for them, and re-layouts, prefix(): return lax.fori_loop(0, ahead, one, state)  49.6 us
    psum x1, waiting for transfers between devices, local(): lax.psum(partial_read.astype(jnp.bfloat16), 'inner').astype(jnp.float32)  44.8 us
    reduce_scatter x1, waiting for transfers between devices, local(): lax.psum_scatter(jnp.dot(rows_part, tangent_load, preferred_element_type=...  44.1 us
    reduce_scatter x1, waiting for transfers between devices, local(): lax.psum_scatter(lax.dot_general(cols_part, adjoint_load, (((0,), (0,)),...  29.7 us
  transfers between devices with their start and end apart: 7, of which 7 were waited for; matrix products, arithmetic and copies ran while one was open for 0% of the time, Pallas kernels for 0%

commit v1 on v0

v1 whole, which is shorter than its diff:
```python
import functools

import jax
import jax.numpy as jnp
from jax import lax
from jax.experimental import pallas as pl
from jax.experimental.pallas import tpu as pltpu
from jax.sharding import PartitionSpec as P

MESH = pl.DeviceIdType.MESH
F32 = jnp.float32
BF16 = jnp.bfloat16

NX = 4
NW = 8
NZ = 8
NK = 2

NN = (((1,), (0,)), ((), ()))
NT = (((1,), (1,)), ((), ()))


def mm(a, b, dims):
    return lax.dot_general(a, b, dims, preferred_element_type=F32)


def kernel(
    load_ref, pivot_ref, transfer_ref, disp_ref, pairs_ref, weights_ref, analysis_hbm, synthesis_hbm,
    out_ref,
    A, S, E, acc, part, own, opp_out, opp_in, mid_out, mid_in, src0, src1,
    blk, gath, shift_out, group_in, zone_in, reply, carry,
    rate_group, rate_zone, tang, read_out, read_in, wread, adj,
    a_sem, s_sem, x_send, x_recv, c_send, c_recv, r_send, r_recv, q_send, q_recv,
):
    storey = lax.axis_index("storey")
    x = lax.axis_index("inner")
    z = lax.div(storey, NW)
    w = lax.rem(storey, NW)
    rows, dofs = load_ref.shape
    cols = rows // 2
    mc = dofs // NK
    lane = cols // NW
    right, left, oppo = lax.rem(x + 1, NX), lax.rem(x + 3, NX), lax.rem(x + 2, NX)
    pending = []

    def xdev(i):
        return (storey, i)

    def wdev(i):
        return (z * NW + i, x)

    def zdev(i):
        return (i * NW + w, x)

    def remote(src, dst, ssem, rsem, dev):
        return pltpu.make_async_remote_copy(
            src_ref=src, dst_ref=dst, send_sem=ssem, recv_sem=rsem, device_id=dev, device_id_type=MESH
        )

    def send(src, dst, ssem, rsem, dev):
        c = remote(src, dst, ssem, rsem, dev)
        c.start()
        pending.append(c)

    def arrive(dst, ssem, rsem, dev):
        remote(dst, dst, ssem, rsem, dev).wait_recv()

    def mode_at(t, k):
        return pl.multiple_of(t * dofs + k * mc, 128)

    a_copies = {}
    for k in range(NK):
        for j, t in enumerate((oppo, right, left, x)):
            at = pl.ds(mode_at(t, k), mc)
            c = pltpu.make_async_copy(analysis_hbm.at[at, :], A.at[at, :], a_sem.at[k * 4 + j])
            c.start()
            a_copies[(k, j)] = c
    s_copy = pltpu.make_async_copy(synthesis_hbm, S, s_sem.at[0])
    s_copy.start()

    barrier = pltpu.get_barrier_semaphore()
    for d in range(1, NX):
        pl.semaphore_signal(barrier, inc=1, device_id=xdev(lax.rem(x + d, NX)), device_id_type=MESH)
    for d in range(1, NW):
        pl.semaphore_signal(barrier, inc=1, device_id=wdev(lax.rem(w + d, NW)), device_id_type=MESH)
    for d in range(1, NZ):
        pl.semaphore_signal(barrier, inc=1, device_id=zdev(lax.rem(z + d, NZ)), device_id_type=MESH)
    pl.semaphore_wait(barrier, NX + NW + NZ - 3)

    t0 = transfer_ref[0:1, :]
    t1 = transfer_ref[1:2, :]
    rate = t0 * t1

    def rates_first():
        rate_group[w] = jnp.broadcast_to(rate, (8, dofs))
        for d in range(1, NW):
            i = lax.rem(w + d, NW)
            send(rate_group.at[w], rate_group.at[w], r_send.at[0, i], r_recv.at[0, w], wdev(i))

    def rates_second():
        for d in range(1, NW):
            i = lax.rem(w + d, NW)
            arrive(rate_group.at[i], r_send.at[0, i], r_recv.at[0, i], wdev(i))
        total = rate_group[0]
        for i in range(1, NW):
            total = total * rate_group[i]
        rate_zone[z] = total
        for d in range(1, NZ):
            i = lax.rem(z + d, NZ)
            send(rate_zone.at[z], rate_zone.at[z], r_send.at[1, i], r_recv.at[1, z], zdev(i))

    def rates_third():
        for d in range(1, NZ):
            i = lax.rem(z + d, NZ)
            arrive(rate_zone.at[i], r_send.at[1, i], r_recv.at[1, i], zdev(i))

    def project(v, k, t, j):
        if v == 0:
            a_copies[(k, j)].wait()
            return mm(load_ref[...], A[pl.ds(mode_at(t, k), mc), :], NT)
        return mm(adj[...], S[:, pl.ds(mode_at(t, k), mc)], NN)

    def rs_opp(v, k):
        opp_out[v, k] = project(v, k, oppo, 0).astype(BF16).reshape(2, cols, mc)
        send(opp_out.at[v, k, 0], opp_in.at[v, k, 0], x_send.at[v, k, 0], x_recv.at[v, k, 0], xdev(right))
        send(opp_out.at[v, k, 1], opp_in.at[v, k, 1], x_send.at[v, k, 1], x_recv.at[v, k, 1], xdev(left))

    def rs_parts(v, k):
        part[0] = project(v, k, right, 1)
        part[1] = project(v, k, left, 2)

    def rs_mid(v, k):
        arrive(opp_in.at[v, k, 0], x_send.at[v, k, 0], x_recv.at[v, k, 0], xdev(left))
        mid_out[v, k, 0, 0:cols] = (part[0, 0:cols] + opp_in[v, k, 0].astype(F32)).astype(BF16)
        mid_out[v, k, 0, cols:rows] = part[0, cols:rows].astype(BF16)
        send(mid_out.at[v, k, 0], mid_in.at[v, k, 0], x_send.at[v, k, 2], x_recv.at[v, k, 2], xdev(right))
        arrive(opp_in.at[v, k, 1], x_send.at[v, k, 1], x_recv.at[v, k, 1], xdev(right))
        mid_out[v, k, 1, 0:cols] = part[1, 0:cols].astype(BF16)
        mid_out[v, k, 1, cols:rows] = (part[1, cols:rows] + opp_in[v, k, 1].astype(F32)).astype(BF16)
        send(mid_out.at[v, k, 1], mid_in.at[v, k, 1], x_send.at[v, k, 3], x_recv.at[v, k, 3], xdev(left))

    def rs_own(v, k):
        own[k] = project(v, k, x, 3)

    def lanes(k):
        return slice(k * mc, (k + 1) * mc)

    def scan_first(v, k):
        arrive(mid_in.at[v, k, 0], x_send.at[v, k, 2], x_recv.at[v, k, 2], xdev(left))
        arrive(mid_in.at[v, k, 1], x_send.at[v, k, 3], x_recv.at[v, k, 3], xdev(right))
        total = own[k] + mid_in[v, k, 0].astype(F32) + mid_in[v, k, 1].astype(F32)
        low, high = total[0:cols], total[cols:rows]
        if v == 0:
            low = low * pivot_ref[0:1, lanes(k)]
            high = high * pivot_ref[1:2, lanes(k)]
            shift = low * t1[:, lanes(k)] + high
        else:
            shift = low * t0[:, lanes(k)] + high * rate[:, lanes(k)]
        src0[k] = low
        src1[k] = high
        shift_out[v, k] = shift.astype(BF16).reshape(NW, lane, mc)
        for d in range(1, NW):
            i = lax.rem(w + d, NW)
            send(shift_out.at[v, k, i], group_in.at[v, k, w], c_send.at[v, k, 0, i], c_recv.at[v, k, 0, w], wdev(i))
        group_in[v, k, w] = shift_out[v, k, w]

    def order(v, n):
        return range(n) if v == 0 else range(n - 1, -1, -1)

    def scan_second(v, k):
        for d in range(1, NW):
            i = lax.rem(w + d, NW)
            arrive(group_in.at[v, k, i], c_send.at[v, k, 0, i], c_recv.at[v, k, 0, i], wdev(i))
        total = None
        for i in order(v, NW):
            term = group_in[v, k, i].astype(F32)
            total = term if total is None else total * rate_group[i, 0:1, lanes(k)] + term
        zone_in[v, k, z] = total.astype(BF16)
        for d in range(1, NZ):
            i = lax.rem(z + d, NZ)
            send(zone_in.at[v, k, z], zone_in.at[v, k, z], c_send.at[v, k, 1, i], c_recv.at[v, k, 1, z], zdev(i))

    def scan_third(v, k):
        for d in range(1, NZ):
            i = lax.rem(z + d, NZ)
            arrive(zone_in.at[v, k, i], c_send.at[v, k, 1, i], c_recv.at[v, k, 1, i], zdev(i))
        state = jnp.zeros((lane, mc), F32)
        for i in order(v, NZ):
            ahead = (i < z) if v == 0 else (i > z)
            state = jnp.where(ahead, state * rate_zone[i, 0:1, lanes(k)] + zone_in[v, k, i].astype(F32), state)
        for i in order(v, NW):
            reply[v, k, i] = state.astype(BF16)
            state = state * rate_group[i, 0:1, lanes(k)] + group_in[v, k, i].astype(F32)
        for d in range(1, NW):
            i = lax.rem(w + d, NW)
            send(reply.at[v, k, i], carry.at[v, k, w], c_send.at[v, k, 2, i], c_recv.at[v, k, 2, w], wdev(i))
        carry[v, k, w] = reply[v, k, w]

    def ag_first(v, k):
        for d in range(1, NW):
            i = lax.rem(w + d, NW)
            arrive(carry.at[v, k, i], c_send.at[v, k, 2, i], c_recv.at[v, k, 2, i], wdev(i))
        state = carry[v, k].reshape(cols, mc).astype(F32)
        if v == 0:
            low = state * t0[:, lanes(k)] + src0[k]
            high = low * t1[:, lanes(k)] + src1[k]
        else:
            high = src1[k] + state
            low = src0[k] + high * t1[:, lanes(k)]
            low = low * pivot_ref[0:1, lanes(k)]
            high = high * pivot_ref[1:2, lanes(k)]
        blk[v, k, 0:cols] = low.astype(BF16)
        blk[v, k, cols:rows] = high.astype(BF16)
        send(blk.at[v, k], gath.at[v, k, 0], x_send.at[v, k, 4], x_recv.at[v, k, 4], xdev(right))
        send(blk.at[v, k], gath.at[v, k, 1], x_send.at[v, k, 5], x_recv.at[v, k, 5], xdev(left))

    def ag_second(v, k):
        lo, hi = pl.ds(0, cols), pl.ds(cols, cols)
        arrive(gath.at[v, k, 0], x_send.at[v, k, 4], x_recv.at[v, k, 4], xdev(left))
        send(gath.at[v, k, 0, lo], gath.at[v, k, 2, lo], x_send.at[v, k, 6], x_recv.at[v, k, 6], xdev(right))
        arrive(gath.at[v, k, 1], x_send.at[v, k, 5], x_recv.at[v, k, 5], xdev(right))
        send(gath.at[v, k, 1, hi], gath.at[v, k, 2, hi], x_send.at[v, k, 7], x_recv.at[v, k, 7], xdev(left))

    def ag_third(v, k):
        lo, hi = pl.ds(0, cols), pl.ds(cols, cols)
        arrive(gath.at[v, k, 2, lo], x_send.at[v, k, 6], x_recv.at[v, k, 6], xdev(left))
        arrive(gath.at[v, k, 2, hi], x_send.at[v, k, 7], x_recv.at[v, k, 7], xdev(right))

    def expand(v, k, t, val):
        if v == 0:
            return mm(val, S[:, pl.ds(mode_at(t, k), mc)], NT)
        return mm(val, A[pl.ds(mode_at(t, k), mc), :], NN)

    def sweep(v):
        rs_opp(v, 0)
        if v == 0:
            rates_first()
        rs_parts(v, 0)
        rs_mid(v, 0)
        rs_own(v, 0)
        rs_opp(v, 1)
        if v == 0:
            rates_second()
        rs_parts(v, 1)
        scan_first(v, 0)
        rs_mid(v, 1)
        rs_own(v, 1)
        scan_second(v, 0)
        if v == 0:
            rates_third()
            build_incidence()
        scan_third(v, 0)
        scan_first(v, 1)
        ag_first(v, 0)
        scan_second(v, 1)
        if v == 0:
            s_copy.wait()
        acc[...] = expand(v, 0, x, blk[v, 0])
        ag_second(v, 0)
        scan_third(v, 1)
        acc[...] += expand(v, 0, left, gath[v, 0, 0]) + expand(v, 0, right, gath[v, 0, 1])
        ag_first(v, 1)
        ag_third(v, 0)
        acc[...] += expand(v, 0, oppo, gath[v, 0, 2]) + expand(v, 1, x, blk[v, 1])
        ag_second(v, 1)
        acc[...] += expand(v, 1, left, gath[v, 1, 0]) + expand(v, 1, right, gath[v, 1, 1])
        ag_third(v, 1)
        acc[...] += expand(v, 1, oppo, gath[v, 1, 2])

    def build_incidence():
        sensors = pairs_ref.shape[1]
        for s in range(2):
            upper = pairs_ref[2 * s : 2 * s + 1, :] - x * dofs
            lower = pairs_ref[2 * s + 1 : 2 * s + 2, :] - x * dofs
            for b in range(0, dofs, 128):
                ids = lax.broadcasted_iota(jnp.int32, (128, sensors), 0) + b
                e = jnp.where(ids == upper, 1.0, 0.0) - jnp.where(ids == lower, 1.0, 0.0)
                E[s, b : b + 128] = e.astype(BF16)

    sweep(0)

    quarter = rows // NX
    for s in range(2):
        tang[s] = acc[s * cols : (s + 1) * cols].astype(BF16)
        r = mm(tang[s], E[s], NN).astype(BF16)
        read_out[2 * s : 2 * s + 2] = r.reshape(2, quarter, r.shape[-1])
    for d in (2, 1, 3):
        i = lax.rem(x + d, NX)
        send(read_out.at[i], read_in.at[x], q_send.at[0, i], q_recv.at[0, x], xdev(i))
    read_in[x] = read_out[x]
    for d in (1, 3, 2):
        i = lax.rem(x + d, NX)
        arrive(read_in.at[i], q_send.at[0, i], q_recv.at[0, i], xdev(i))
    total = read_in[0].astype(F32)
    for i in range(1, NX):
        total = total + read_in[i].astype(F32)
    weight = weights_ref[pl.ds(lax.div(x, 2), 1), :]
    wread[x] = (total * weight).astype(BF16)
    for d in (2, 1, 3):
        i = lax.rem(x + d, NX)
        send(wread.at[x], wread.at[x], q_send.at[1, i], q_recv.at[1, x], xdev(i))
    for d in (1, 3, 2):
        i = lax.rem(x + d, NX)
        arrive(wread.at[i], q_send.at[1, i], q_recv.at[1, i], xdev(i))
    for s in range(2):
        r = wread[2 * s : 2 * s + 2].reshape(cols, wread.shape[-1])
        adj[s * cols : (s + 1) * cols] = mm(r, E[s], NT).astype(BF16)

    sweep(1)

    for s in range(2):
        at = slice(s * cols, (s + 1) * cols)
        out_ref[at] = -disp_ref[s : s + 1, :] * acc[at]
    for c in pending:
        c.wait_send()


def chain(load, pivot, transfer, disp, pairs, weights, analysis, synthesis):
    rows, dofs = load.shape
    modes = analysis.shape[0]
    cols = rows // 2
    mc = dofs // NK
    lane = cols // NW
    sensors = pairs.shape[1]
    vm = pltpu.VMEM
    dma = pltpu.SemaphoreType.DMA
    scratch = [
        vm((modes, dofs), BF16),
        vm((dofs, modes), BF16),
        vm((2, dofs, sensors), BF16),
        vm((rows, dofs), F32),
        vm((2, rows, mc), F32),
        vm((NK, rows, mc), F32),
        vm((2, NK, 2, cols, mc), BF16),
        vm((2, NK, 2, cols, mc), BF16),
        vm((2, NK, 2, rows, mc), BF16),
        vm((2, NK, 2, rows, mc), BF16),
        vm((NK, cols, mc), F32),
        vm((NK, cols, mc), F32),
        vm((2, NK, rows, mc), BF16),
        vm((2, NK, 3, rows, mc), BF16),
        vm((2, NK, NW, lane, mc), BF16),
        vm((2, NK, NW, lane, mc), BF16),
        vm((2, NK, NZ, lane, mc), BF16),
        vm((2, NK, NW, lane, mc), BF16),
        vm((2, NK, NW, lane, mc), BF16),
        vm((NW, 8, dofs), F32),
        vm((NZ, 8, dofs), F32),
        vm((2, cols, dofs), BF16),
        vm((NX, rows // NX, sensors), BF16),
        vm((NX, rows // NX, sensors), BF16),
        vm((NX, rows // NX, sensors), BF16),
        vm((rows, dofs), BF16),
        dma((8,)), dma((1,)),
        dma((2, NK, 8)), dma((2, NK, 8)),
        dma((2, NK, 3, 8)), dma((2, NK, 3, 8)),
        dma((2, 8)), dma((2, 8)),
        dma((2, 4)), dma((2, 4)),
    ]
    in_vmem = pl.BlockSpec(memory_space=pltpu.VMEM)
    in_hbm = pl.BlockSpec(memory_space=pl.ANY)
    return pl.pallas_call(
        kernel,
        out_shape=jax.ShapeDtypeStruct((rows, dofs), F32),
        in_specs=[in_vmem] * 6 + [in_hbm] * 2,
        out_specs=in_vmem,
        scratch_shapes=scratch,
        compiler_params=pltpu.CompilerParams(
            collective_id=0, has_side_effects=True, vmem_limit_bytes=56 * 1024 * 1024
        ),
        cost_estimate=pl.CostEstimate(
            flops=8 * rows * modes * dofs, bytes_accessed=4 * modes * dofs, transcendentals=0
        ),
        name="chain",
    )(load, pivot, transfer, disp, pairs, weights, analysis, synthesis)


def local(synthesis, analysis, pivot, transfer, displacement, directions, sensor_pairs, sensor_weights):
    dofs, storeys, columns = directions.shape
    load = (-(displacement.T[:, :, None] * directions.astype(F32))).astype(BF16)
    load = load.transpose(1, 2, 0).reshape(storeys * columns, dofs)
    pairs = sensor_pairs.transpose(0, 2, 1).reshape(2 * storeys, -1)
    out = chain(load, pivot, transfer, displacement, pairs, sensor_weights, analysis, synthesis)
    return out.reshape(storeys, columns, dofs).transpose(2, 0, 1)


def solution(mesh):
    return jax.shard_map(
        local,
        mesh=mesh,
        in_specs=(
            P("inner", None),
            P(None, "inner"),
            P("storey", "inner"),
            P("storey", "inner"),
            P("storey", "inner"),
            P("inner", "storey", None),
            P("storey", None, None),
            P("storey", None),
        ),
        out_specs=P("inner", "storey", None),
        check_vma=False,
    )
```

time: 670 us -> 125 us (0.19)
  waiting for transfers between devices: 393 us -> 0 us
  Pallas kernels: 0 us -> 118 us
  blocking collectives: 92.1 us -> 0 us
  other arithmetic: 85.8 us -> 1.91 us
  local copies, waits for them, and re-layouts: 54.2 us -> 5.3 us
  matrix products: 24.6 us -> 0 us
  between operations: 13.8 us -> 0.03 us
    all_gather x4 -> x0, waiting for transfers between devices: 274 us -> none  [the longest x2 151 us: prefix(): gathered = jax.tree.map(lambda a: lax.all_gather(a, axis), part)]
    pallas_call x0 -> x1, Pallas kernels: none -> 118 us  [chain(): pl.pallas_call(kernel, out_shape=jax.ShapeDtypeStruct((rows, dofs), F32),...]
    all_gather x2 -> x0, blocking collectives: 92.1 us -> none  [prefix(): gathered = jax.tree.map(lambda a: lax.all_gather(a, axis), part)]
    add x70 -> x0, other arithmetic: 76.1 us -> none  [the longest x63 74.4 us: affine(): rate_late[..., None] * shift_early + shift_late]
    reduce_scatter x2 -> x0, waiting for transfers between devices: 73.8 us -> none  [the longest x1 44.1 us: local(): lax.psum_scatter(jnp.dot(rows_part, tangent_load, preferred_element_type=...]
    while x4 -> x0, local copies, waits for them, and re-layouts: 49.6 us -> none  [prefix(): return lax.fori_loop(0, ahead, one, state)]
    psum x1 -> x0, waiting for transfers between devices: 44.8 us -> none  [local(): lax.psum(partial_read.astype(jnp.bfloat16), 'inner').astype(jnp.float32)]
    dot_general x8 -> x0, matrix products: 24.6 us -> none  [the longest x1 5.42 us: local(): jnp.dot(rows_part, tangent_load, preferred_element_type=jnp.float32)]
  transfers between devices with their start and end apart: 7 -> 0, of which waited for: 7 -> 0; matrix products, arithmetic and copies ran while one was open for 0% -> 0% of each run, Pallas kernels for 0% -> 0%
where the time goes in v1:
time: 125 us
  Pallas kernels  118 us (94%)
  local copies, waits for them, and re-layouts  5.3 us (4%)
  other arithmetic  1.91 us (2%)
    pallas_call x1, Pallas kernels, chain(): pl.pallas_call(kernel, out_shape=jax.ShapeDtypeStruct((rows, dofs), F32),...  118 us

profile of v1, /device:TPU:1, one launch (start us, length us, event | category | flops | bytes accessed | tf_op | source)
XLA Modules:
  0.0 125.1 jit_solution(11684465562296662878)
XLA Ops:
  0.0 1.3 %reshape.11.pairs_ref = s32[4,512]{1,0:T(4,128)} reshape(s32[2,2,512]{2,1,0:T(2,128)} %bitcast.9) | data formatting | bytes 16384 | tf_op jit(solution)/shard_map/reshape | solution.py:382
  1.3 0.9 copy.9
  2.2 1.9 %fusion = bf16[2,128,768]{1,0,2:T(2,128)(2,1)S(1)} fusion(bf16[768,2,128]{2,1,0:T(2,128)(2,1)} %param.13, f32[768,2]{1,0:T(8,128)S(1)} %copy.9), kind=kLoop, calls=%fused_computation.1 | loop fusion | flops 786432 | bytes 792576 | tf_op jit(solution)/shard_map/transpose | solution.py:381
  4.1 1.0 copy.10
  5.1 117.9 %chain.1 = f32[256,768]{1,0:T(8,128)} custom-call(bf16[256,768]{1,0:T(8,128)(2,1)} %bitcast.8, f32[2,768]{1,0:T(2,128)} %pivot_ref.1, f32[2,768]{1,0:T(2,128)} %transfer_ref.1, f32[2,768]{1,0:T(2,128)} %disp_ref.1, s32[4,512]{1,0:T(4,128)} %reshape.11.pairs_ref, f32[2,512]{1,0:T(2,128)} %weights_ref.1, bf16[3072,768]{1,0:T(8,128)(2,1)} %analysis_hbm.1, ...), custom_call_target="tpu_custom_call" | custom-call | flops 4831838208 | bytes 9437184 | tf_op jit(solution)/shard_map/chain/pallas_call | solution.py:362
  123.0 2.1 %copy.11 = f32[2,128,768]{1,0,2:T(2,128)} copy(f32[2,128,768]{2,1,0:T(8,128)} %bitcast.7) | data formatting | bytes 1572864 | tf_op jit(solution)/shard_map/reshape | solution.py:384

commit v2 on v1

v2 whole, which is shorter than its diff:
```python
import jax
import jax.numpy as jnp
from jax import lax
from jax.experimental import pallas as pl
from jax.experimental.pallas import tpu as pltpu
from jax.sharding import PartitionSpec as P

MESH = pl.DeviceIdType.MESH
F32 = jnp.float32
BF16 = jnp.bfloat16

NX = 4
NW = 8
NZ = 8
CHUNKS = ((0, 384), (384, 384))
NK = len(CHUNKS)

NN = (((1,), (0,)), ((), ()))
NT = (((1,), (1,)), ((), ()))


def mm(a, b, dims):
    return lax.dot_general(a, b, dims, preferred_element_type=F32)


def kernel(
    load_ref, pivot_ref, transfer_ref, disp_ref, pairs_ref, weights_ref, analysis_hbm, synthesis_hbm,
    out_ref,
    A, S, E, acc, part, opp_out, opp_in, mid_out, mid_in, loc, gath, car, cgath,
    shift, group_in, zone_in, reply, coef, rate_group, rate_zone,
    tang, read_out, read_in, wread, adj,
    a_sem, s_sem, x_send, x_recv, k_send, k_recv, c_send, c_recv, r_send, r_recv, q_send, q_recv,
):
    storey = lax.axis_index("storey")
    x = lax.axis_index("inner")
    z = lax.div(storey, NW)
    w = lax.rem(storey, NW)
    rows, dofs = load_ref.shape
    cols = rows // 2
    half = cols // 2
    lane = cols // NW
    right, left, oppo = lax.rem(x + 1, NX), lax.rem(x + 3, NX), lax.rem(x + 2, NX)
    pending = []

    def xdev(i):
        return (storey, i)

    def wdev(i):
        return (z * NW + i, x)

    def zdev(i):
        return (i * NW + w, x)

    def remote(src, dst, ssem, rsem, dev):
        return pltpu.make_async_remote_copy(
            src_ref=src, dst_ref=dst, send_sem=ssem, recv_sem=rsem, device_id=dev, device_id_type=MESH
        )

    def send(src, dst, ssem, rsem, dev):
        c = remote(src, dst, ssem, rsem, dev)
        c.start()
        pending.append(c)

    def arrive(dst, ssem, rsem, dev):
        remote(dst, dst, ssem, rsem, dev).wait_recv()

    def lanes(k):
        return pl.ds(CHUNKS[k][0], CHUNKS[k][1])

    def block(t):
        return pl.ds(pl.multiple_of(t * dofs, 128), dofs)

    def modes(t, k):
        return pl.ds(pl.multiple_of(t * dofs + CHUNKS[k][0], 128), CHUNKS[k][1])

    targets = (oppo, right, left, x)
    a_copies = []
    for j, t in enumerate(targets):
        c = pltpu.make_async_copy(analysis_hbm.at[block(t), :], A.at[block(t), :], a_sem.at[j])
        c.start()
        a_copies.append(c)
    s_copy = pltpu.make_async_copy(synthesis_hbm, S, s_sem.at[0])
    s_copy.start()

    barrier = pltpu.get_barrier_semaphore()
    for d in range(1, NX):
        pl.semaphore_signal(barrier, inc=1, device_id=xdev(lax.rem(x + d, NX)), device_id_type=MESH)
    for d in range(1, NW):
        pl.semaphore_signal(barrier, inc=1, device_id=wdev(lax.rem(w + d, NW)), device_id_type=MESH)
    for d in range(1, NZ):
        pl.semaphore_signal(barrier, inc=1, device_id=zdev(lax.rem(z + d, NZ)), device_id_type=MESH)

    t0, t1 = transfer_ref[0:1, :], transfer_ref[1:2, :]
    p0, p1 = pivot_ref[0:1, :], pivot_ref[1:2, :]
    for n, row in enumerate((t0, t1, p0, p1, t0 * t1, t1 * p0, t0, t1)):
        coef[x, n : n + 1] = row

    def coefficients_first():
        for d in (2, 1, 3):
            i = lax.rem(x + d, NX)
            send(coef.at[x], coef.at[x], k_send.at[2, 0, i], k_recv.at[2, 0, x], xdev(i))

    def coefficients_second():
        for d in (1, 3, 2):
            i = lax.rem(x + d, NX)
            arrive(coef.at[i], k_send.at[2, 0, i], k_recv.at[2, 0, i], xdev(i))

    def rates_first():
        rate_group[w] = jnp.broadcast_to(t0 * t1, (8, dofs))
        for d in range(1, NW):
            i = lax.rem(w + d, NW)
            send(rate_group.at[w], rate_group.at[w], r_send.at[0, i], r_recv.at[0, w], wdev(i))

    def rates_second():
        for d in range(1, NW):
            i = lax.rem(w + d, NW)
            arrive(rate_group.at[i], r_send.at[0, i], r_recv.at[0, i], wdev(i))
        total = rate_group[0]
        for i in range(1, NW):
            total = total * rate_group[i]
        rate_zone[z] = total
        for d in range(1, NZ):
            i = lax.rem(z + d, NZ)
            send(rate_zone.at[z], rate_zone.at[z], r_send.at[1, i], r_recv.at[1, z], zdev(i))

    def rates_third():
        for d in range(1, NZ):
            i = lax.rem(z + d, NZ)
            arrive(rate_zone.at[i], r_send.at[1, i], r_recv.at[1, i], zdev(i))

    def build_incidence():
        sensors = pairs_ref.shape[2]
        for s in range(2):
            upper = pairs_ref[s, 0:1, :] - x * dofs
            lower = pairs_ref[s, 1:2, :] - x * dofs
            for b in range(0, dofs, 128):
                ids = lax.broadcasted_iota(jnp.int32, (128, sensors), 0) + b
                e = jnp.where(ids == upper, 1.0, 0.0) - jnp.where(ids == lower, 1.0, 0.0)
                E[s, b : b + 128] = e.astype(BF16)

    def project(v, j):
        t = targets[j]
        if v == 0:
            a_copies[j].wait()
            part[j] = mm(load_ref[...], A[block(t), :], NT)
        else:
            part[j] = mm(adj[...], S[:, block(t)], NN)

    def term(v, q, k, j, lo=0, n=cols):
        t = targets[j]
        low = part[j, lo : lo + n, lanes(k)]
        high = part[j, cols + lo : cols + lo + n, lanes(k)]
        if q == 1:
            return low if v == 0 else high
        if v == 0:
            return low * coef[t, 5:6, lanes(k)] + high * coef[t, 3:4, lanes(k)]
        return low + high * coef[t, 1:2, lanes(k)]

    def rs_opp(v, q, k):
        for n, dev in ((0, right), (1, left)):
            opp_out[v, q, n, :, lanes(k)] = term(v, q, k, 0, n * half, half).astype(BF16)
            send(
                opp_out.at[v, q, n, :, lanes(k)], opp_in.at[v, q, n, :, lanes(k)],
                x_send.at[v, q, k, n], x_recv.at[v, q, k, n], xdev(dev),
            )

    def rs_mid(v, q, k):
        for n, dev, back in ((0, right, left), (1, left, right)):
            arrive(opp_in.at[v, q, n, :, lanes(k)], x_send.at[v, q, k, n], x_recv.at[v, q, k, n], xdev(back))
            own, other = pl.ds(n * half, half), pl.ds((1 - n) * half, half)
            mine = term(v, q, k, 1 + n, n * half, half) + opp_in[v, q, n, :, lanes(k)].astype(F32)
            mid_out[v, q, n, own, lanes(k)] = mine.astype(BF16)
            mid_out[v, q, n, other, lanes(k)] = term(v, q, k, 1 + n, (1 - n) * half, half).astype(BF16)
            send(
                mid_out.at[v, q, n, :, lanes(k)], mid_in.at[v, q, n, :, lanes(k)],
                x_send.at[v, q, k, 2 + n], x_recv.at[v, q, k, 2 + n], xdev(dev),
            )

    def rs_end(v, q, k):
        for n, back in ((0, left), (1, right)):
            arrive(
                mid_in.at[v, q, n, :, lanes(k)], x_send.at[v, q, k, 2 + n], x_recv.at[v, q, k, 2 + n], xdev(back)
            )
        total = term(v, q, k, 3) + mid_in[v, q, 0, :, lanes(k)].astype(F32) + mid_in[v, q, 1, :, lanes(k)].astype(F32)
        if q == 0:
            out = total if v == 0 else total * coef[x, 0:1, lanes(k)]
            shift[v, :, :, lanes(k)] = out.astype(BF16).reshape(NW, lane, CHUNKS[k][1])
            for d in range(1, NW):
                i = lax.rem(w + d, NW)
                send(
                    shift.at[v, i, :, lanes(k)], group_in.at[v, w, :, lanes(k)],
                    c_send.at[v, k, 0, i], c_recv.at[v, k, 0, w], wdev(i),
                )
            group_in[v, w, :, lanes(k)] = shift[v, w, :, lanes(k)]
            if v == 1:
                total = total * coef[x, 2:3, lanes(k)]
        else:
            total = total * (coef[x, 2:3, lanes(k)] if v == 0 else coef[x, 3:4, lanes(k)])
        loc[v, q, :, lanes(k)] = total.astype(BF16)
        for n, dev in ((0, right), (1, left)):
            send(
                loc.at[v, q, :, lanes(k)], gath.at[v, q, n, :, lanes(k)],
                x_send.at[v, q, k, 4 + n], x_recv.at[v, q, k, 4 + n], xdev(dev),
            )

    def ag_second(v, q, k):
        for n, dev, back in ((0, right, left), (1, left, right)):
            arrive(gath.at[v, q, n, :, lanes(k)], x_send.at[v, q, k, 4 + n], x_recv.at[v, q, k, 4 + n], xdev(back))
            at = pl.ds(n * half, half)
            send(
                gath.at[v, q, n, at, lanes(k)], gath.at[v, q, 2, at, lanes(k)],
                x_send.at[v, q, k, 6 + n], x_recv.at[v, q, k, 6 + n], xdev(dev),
            )

    def ag_third(v, q, k):
        for n, back in ((0, left), (1, right)):
            at = pl.ds(n * half, half)
            arrive(gath.at[v, q, 2, at, lanes(k)], x_send.at[v, q, k, 6 + n], x_recv.at[v, q, k, 6 + n], xdev(back))

    def order(v, n):
        return range(n) if v == 0 else range(n - 1, -1, -1)

    def scan_second(v, k):
        for d in range(1, NW):
            i = lax.rem(w + d, NW)
            arrive(group_in.at[v, i, :, lanes(k)], c_send.at[v, k, 0, i], c_recv.at[v, k, 0, i], wdev(i))
        total = None
        for i in order(v, NW):
            new = group_in[v, i, :, lanes(k)].astype(F32)
            total = new if total is None else total * rate_group[i, 0:1, lanes(k)] + new
        zone_in[v, z, :, lanes(k)] = total.astype(BF16)
        for d in range(1, NZ):
            i = lax.rem(z + d, NZ)
            send(
                zone_in.at[v, z, :, lanes(k)], zone_in.at[v, z, :, lanes(k)],
                c_send.at[v, k, 1, i], c_recv.at[v, k, 1, z], zdev(i),
            )

    def scan_third(v, k):
        for d in range(1, NZ):
            i = lax.rem(z + d, NZ)
            arrive(zone_in.at[v, i, :, lanes(k)], c_send.at[v, k, 1, i], c_recv.at[v, k, 1, i], zdev(i))
        state = jnp.zeros((lane, CHUNKS[k][1]), F32)
        for i in order(v, NZ):
            ahead = (i < z) if v == 0 else (i > z)
            new = state * rate_zone[i, 0:1, lanes(k)] + zone_in[v, i, :, lanes(k)].astype(F32)
            state = jnp.where(ahead, new, state)
        for i in order(v, NW):
            reply[v, i, :, lanes(k)] = state.astype(BF16)
            state = state * rate_group[i, 0:1, lanes(k)] + group_in[v, i, :, lanes(k)].astype(F32)
        for d in range(1, NW):
            i = lax.rem(w + d, NW)
            send(
                reply.at[v, i, :, lanes(k)], car.at[v, w, :, lanes(k)],
                c_send.at[v, k, 2, i], c_recv.at[v, k, 2, w], wdev(i),
            )
        car[v, w, :, lanes(k)] = reply[v, w, :, lanes(k)]

    def carry_first(v, k):
        for d in range(1, NW):
            i = lax.rem(w + d, NW)
            arrive(car.at[v, i, :, lanes(k)], c_send.at[v, k, 2, i], c_recv.at[v, k, 2, i], wdev(i))
        for n, dev in ((2, oppo), (0, right), (1, left)):
            send(
                car.at[v, :, :, lanes(k)], cgath.at[v, n, :, :, lanes(k)],
                k_send.at[v, k, n], k_recv.at[v, k, n], xdev(dev),
            )

    def expand(v, k, n, first=False):
        t = (left, right, oppo, x)[n]
        width = CHUNKS[k][1]
        if n < 3:
            arrive(cgath.at[v, n, :, :, lanes(k)], k_send.at[v, k, n], k_recv.at[v, k, n], xdev(t))
            c = cgath[v, n, :, :, lanes(k)]
            lead, rest = gath[v, 0, n, :, lanes(k)], gath[v, 1, n, :, lanes(k)]
        else:
            c = car[v, :, :, lanes(k)]
            lead, rest = loc[v, 0, :, lanes(k)], loc[v, 1, :, lanes(k)]
        c = c.reshape(cols, width).astype(F32)
        lead, rest = lead.astype(F32), rest.astype(F32)
        if v == 0:
            low = rest + c * coef[t, 0:1, lanes(k)]
            high = lead + c * coef[t, 4:5, lanes(k)]
        else:
            low = lead + c * coef[t, 5:6, lanes(k)]
            high = rest + c * coef[t, 3:4, lanes(k)]
        val = jnp.concatenate([low.astype(BF16), high.astype(BF16)], axis=0)
        if v == 0:
            new = mm(val, S[:, modes(t, k)], NT)
        else:
            new = mm(val, A[modes(t, k), :], NN)
        acc[...] = new if first else acc[...] + new

    def sweep(v):
        if v == 0:
            project(0, 0)
            project(0, 1)
            pl.semaphore_wait(barrier, NX + NW + NZ - 3)
            coefficients_first()
            for k in range(NK):
                rs_opp(0, 1, k)
            rates_first()
            project(0, 2)
            project(0, 3)
            build_incidence()
            coefficients_second()
            for k in range(NK):
                rs_opp(0, 0, k)
            rs_mid(0, 1, 0)
            rates_second()
            for k in range(NK):
                rs_mid(0, 0, k)
            for k in range(1, NK):
                rs_mid(0, 1, k)
        else:
            project(1, 0)
            for q in range(2):
                for k in range(NK):
                    rs_opp(1, q, k)
            for j in range(1, 4):
                project(1, j)
            for q in range(2):
                for k in range(NK):
                    rs_mid(1, q, k)
        rs_end(v, 0, 0)
        rs_end(v, 0, 1)
        rs_end(v, 1, 0)
        scan_second(v, 0)
        rs_end(v, 1, 1)
        if v == 0:
            rates_third()
            s_copy.wait()
        scan_second(v, 1)
        ag_second(v, 0, 0)
        scan_third(v, 0)
        ag_second(v, 0, 1)
        scan_third(v, 1)
        ag_second(v, 1, 0)
        ag_second(v, 1, 1)
        carry_first(v, 0)
        carry_first(v, 1)
        expand(v, 0, 3, True)
        expand(v, 1, 3)
        for k in range(NK):
            expand(v, k, 0)
            expand(v, k, 1)
            for q in range(2):
                ag_third(v, q, k)
            expand(v, k, 2)

    sweep(0)

    quarter = rows // NX
    for s in range(2):
        tang[s] = acc[s * cols : (s + 1) * cols].astype(BF16)
        r = mm(tang[s], E[s], NN).astype(BF16)
        read_out[2 * s : 2 * s + 2] = r.reshape(2, quarter, r.shape[-1])
    for d in (2, 1, 3):
        i = lax.rem(x + d, NX)
        send(read_out.at[i], read_in.at[x], q_send.at[0, i], q_recv.at[0, x], xdev(i))
    read_in[x] = read_out[x]
    for d in (1, 3, 2):
        i = lax.rem(x + d, NX)
        arrive(read_in.at[i], q_send.at[0, i], q_recv.at[0, i], xdev(i))
    total = read_in[0].astype(F32)
    for i in range(1, NX):
        total = total + read_in[i].astype(F32)
    weight = weights_ref[pl.ds(lax.div(x, 2), 1), :]
    wread[x] = (total * weight).astype(BF16)
    for d in (2, 1, 3):
        i = lax.rem(x + d, NX)
        send(wread.at[x], wread.at[x], q_send.at[1, i], q_recv.at[1, x], xdev(i))
    for d in (1, 3, 2):
        i = lax.rem(x + d, NX)
        arrive(wread.at[i], q_send.at[1, i], q_recv.at[1, i], xdev(i))
    for s in range(2):
        r = wread[2 * s : 2 * s + 2].reshape(cols, wread.shape[-1])
        adj[s * cols : (s + 1) * cols] = mm(r, E[s], NT).astype(BF16)

    sweep(1)

    for s in range(2):
        at = slice(s * cols, (s + 1) * cols)
        out_ref[at] = -disp_ref[s : s + 1, :] * acc[at]
    for c in pending:
        c.wait_send()


def chain(load, pivot, transfer, disp, pairs, weights, analysis, synthesis):
    rows, dofs = load.shape
    modes = analysis.shape[0]
    cols = rows // 2
    lane = cols // NW
    sensors = pairs.shape[2]
    vm = pltpu.VMEM
    dma = pltpu.SemaphoreType.DMA
    scratch = [
        vm((modes, dofs), BF16),
        vm((dofs, modes), BF16),
        vm((2, dofs, sensors), BF16),
        vm((rows, dofs), F32),
        vm((4, rows, dofs), F32),
        vm((2, 2, 2, cols // 2, dofs), BF16),
        vm((2, 2, 2, cols // 2, dofs), BF16),
        vm((2, 2, 2, cols, dofs), BF16),
        vm((2, 2, 2, cols, dofs), BF16),
        vm((2, 2, cols, dofs), BF16),
        vm((2, 2, 3, cols, dofs), BF16),
        vm((2, NW, lane, dofs), BF16),
        vm((2, 3, NW, lane, dofs), BF16),
        vm((2, NW, lane, dofs), BF16),
        vm((2, NW, lane, dofs), BF16),
        vm((2, NZ, lane, dofs), BF16),
        vm((2, NW, lane, dofs), BF16),
        vm((NX, 8, dofs), F32),
        vm((NW, 8, dofs), F32),
        vm((NZ, 8, dofs), F32),
        vm((2, cols, dofs), BF16),
        vm((NX, rows // NX, sensors), BF16),
        vm((NX, rows // NX, sensors), BF16),
        vm((NX, rows // NX, sensors), BF16),
        vm((rows, dofs), BF16),
        dma((4,)), dma((1,)),
        dma((2, 2, NK, 8)), dma((2, 2, NK, 8)),
        dma((3, NK, 4)), dma((3, NK, 4)),
        dma((2, NK, 3, 8)), dma((2, NK, 3, 8)),
        dma((2, 8)), dma((2, 8)),
        dma((2, 4)), dma((2, 4)),
    ]
    in_vmem = pl.BlockSpec(memory_space=pltpu.VMEM)
    in_hbm = pl.BlockSpec(memory_space=pl.ANY)
    return pl.pallas_call(
        kernel,
        out_shape=jax.ShapeDtypeStruct((rows, dofs), F32),
        in_specs=[in_vmem] * 6 + [in_hbm] * 2,
        out_specs=in_vmem,
        scratch_shapes=scratch,
        compiler_params=pltpu.CompilerParams(
            collective_id=0, has_side_effects=True, vmem_limit_bytes=56 * 1024 * 1024
        ),
        cost_estimate=pl.CostEstimate(
            flops=8 * rows * modes * dofs, bytes_accessed=4 * modes * dofs, transcendentals=0
        ),
        name="chain",
    )(load, pivot, transfer, disp, pairs, weights, analysis, synthesis)


def local(synthesis, analysis, pivot, transfer, displacement, directions, sensor_pairs, sensor_weights):
    dofs, storeys, columns = directions.shape
    load = (-(displacement.T[:, :, None] * directions.astype(F32))).astype(BF16)
    load = load.transpose(1, 2, 0).reshape(storeys * columns, dofs)
    pairs = sensor_pairs.transpose(0, 2, 1)
    out = chain(load, pivot, transfer, displacement, pairs, sensor_weights, analysis, synthesis)
    return out.reshape(storeys, columns, dofs).transpose(2, 0, 1)


def solution(mesh):
    return jax.shard_map(
        local,
        mesh=mesh,
        in_specs=(
            P("inner", None),
            P(None, "inner"),
            P("storey", "inner"),
            P("storey", "inner"),
            P("storey", "inner"),
            P("inner", "storey", None),
            P("storey", None, None),
            P("storey", None),
        ),
        out_specs=P("inner", "storey", None),
        check_vma=False,
    )
```

time: 125 us -> 109 us (0.87); the launches traced: 125 us -> 107 us
  Pallas kernels: 118 us -> 101 us
  local copies, waits for them, and re-layouts: 5.3 us -> 4.01 us
    pallas_call x1, Pallas kernels: 118 us -> 101 us  [chain(): pl.pallas_call(kernel, out_shape=jax.ShapeDtypeStruct((rows, dofs), F32),...]
    reshape x1 -> x0, local copies, waits for them, and re-layouts: 1.3 us -> none  [local(): pairs = sensor_pairs.transpose(0, 2, 1).reshape(2 * storeys, -1)]
where the time goes in v2:
time: 109 us; the launch traced here: 107 us
  Pallas kernels  101 us (93%)
  local copies, waits for them, and re-layouts  4.01 us (4%)
  other arithmetic  1.91 us (2%)
    pallas_call x1, Pallas kernels, chain(): pl.pallas_call(kernel, out_shape=jax.ShapeDtypeStruct((rows, dofs), F32),...  101 us

profile of v2, /device:TPU:1, one launch (start us, length us, event | category | flops | bytes accessed | tf_op | source)
XLA Modules:
  0.0 107.2 jit_solution(4201794343962614297)
XLA Ops:
  0.0 0.9 copy.9
  0.9 1.9 %fusion = bf16[2,128,768]{1,0,2:T(2,128)(2,1)S(1)} fusion(bf16[768,2,128]{2,1,0:T(2,128)(2,1)} %param.13, f32[768,2]{1,0:T(8,128)S(1)} %copy.9), kind=kLoop, calls=%fused_computation.1 | loop fusion | flops 786432 | bytes 792576 | tf_op jit(solution)/shard_map/transpose | solution.py:451
  2.8 1.0 copy.10
  3.8 101.3 %chain.1 = f32[256,768]{1,0:T(8,128)} custom-call(bf16[256,768]{1,0:T(8,128)(2,1)} %bitcast.8, f32[2,768]{1,0:T(2,128)} %pivot_ref.1, f32[2,768]{1,0:T(2,128)} %transfer_ref.1, f32[2,768]{1,0:T(2,128)} %disp_ref.1, s32[2,2,512]{2,1,0:T(2,128)} %bitcast.10, f32[2,512]{1,0:T(2,128)} %weights_ref.1, bf16[3072,768]{1,0:T(8,128)(2,1)} %analysis_hbm.1, ...), custom_call_target="tpu_custom_call" | custom-call | flops 4831838208 | bytes 9437184 | tf_op jit(solution)/shard_map/chain/pallas_call | solution.py:432
  105.2 2.1 %copy.11 = f32[2,128,768]{1,0,2:T(2,128)} copy(f32[2,128,768]{2,1,0:T(8,128)} %bitcast.7) | data formatting | bytes 1572864 | tf_op jit(solution)/shard_map/reshape | solution.py:454

commit v3 on v2

v3 whole, which is shorter than its diff:
```python
import jax
import jax.numpy as jnp
from jax import lax
from jax.experimental import pallas as pl
from jax.experimental.pallas import tpu as pltpu
from jax.sharding import PartitionSpec as P

MESH = pl.DeviceIdType.MESH
F32 = jnp.float32
BF16 = jnp.bfloat16

NX = 4
NW = 8
NZ = 8
NU = 2

NN = (((1,), (0,)), ((), ()))
NT = (((1,), (1,)), ((), ()))

ORDER = (
    "INC", "P002", "P001", "BAR", "COEF1", "RATE1", "P000", "OPP000", "OPP001", "P003", "P013", "P010", "OPP010",
    "OPP011", "P012", "P011", "COEF2", "RATE2", "MID000", "MID001", "MID010", "MID011", "END000", "RATE3", "END001",
    "END010", "END011", "SC200", "AG200", "SC201", "AG201", "SC300", "SC301", "CAR00", "EXP00", "CAR01", "EXP01",
    "EXQ00", "SEN10", "EXQ01", "SEN11", "SEN20", "SEN21", "ADJ0", "P100", "OPP100", "P102", "P103", "P101",
    "OPP101", "ADJ1", "P110", "OPP110", "MID100", "P111", "P112", "OPP111", "P113", "MID101", "MID110", "END100",
    "MID111", "END101", "SC210", "END110", "END111", "AG210", "SC211", "SC310", "AG211", "CAR10", "SC311", "EXP10",
    "CAR11", "EXP11", "EXQ10", "OUT0", "EXQ11", "OUT1",
)


def mm(a, b, dims):
    return lax.dot_general(a, b, dims, preferred_element_type=F32)


def kernel(
    load_ref, pivot_ref, transfer_ref, disp_ref, pairs_ref, weights_ref, analysis_hbm, synthesis_hbm,
    out_ref,
    A, S, E, acc, part, keep, opp_out, opp_in, mid_out, mid_in, early, early_in, late, late_in,
    shift, group_in, zone_in, reply, car, coef, rate_group, rate_zone,
    read_out, read_in, wread, adj,
    a_sem, s_sem, x_send, x_recv, k_send, k_recv, c_send, c_recv, r_send, r_recv, q_send, q_recv,
):
    storey = lax.axis_index("storey")
    x = lax.axis_index("inner")
    z = lax.div(storey, NW)
    w = lax.rem(storey, NW)
    rows, dofs = load_ref.shape
    cols = rows // 2
    hc = cols // NU
    half = hc // 2
    lane = 2 * hc // NW
    hm = dofs // 2
    right, left, oppo = lax.rem(x + 1, NX), lax.rem(x + 3, NX), lax.rem(x + 2, NX)
    pending = []

    def xdev(i):
        return (storey, i)

    def wdev(i):
        return (z * NW + i, x)

    def zdev(i):
        return (i * NW + w, x)

    def remote(src, dst, ssem, rsem, dev):
        return pltpu.make_async_remote_copy(
            src_ref=src, dst_ref=dst, send_sem=ssem, recv_sem=rsem, device_id=dev, device_id_type=MESH
        )

    def send(src, dst, ssem, rsem, dev):
        c = remote(src, dst, ssem, rsem, dev)
        c.start()
        pending.append(c)

    def arrive(dst, ssem, rsem, dev):
        remote(dst, dst, ssem, rsem, dev).wait_recv()

    def peers(me, n):
        return [lax.rem(me + d, n) for d in range(1, n)]

    xpeers, wpeers, zpeers = [oppo, right, left], peers(w, NW), peers(z, NZ)

    def block(t):
        return pl.ds(pl.multiple_of(t * dofs, 128), dofs)

    targets = (oppo, right, left, x)
    a_copies = {}
    for j in (0, 1, 2, 3):
        at = block(targets[j])
        c = pltpu.make_async_copy(analysis_hbm.at[at, :], A.at[at, :], a_sem.at[j])
        c.start()
        a_copies[j] = c
    s_copies = [pltpu.make_async_copy(synthesis_hbm, S, s_sem.at[0])]
    s_copies[0].start()

    barrier = pltpu.get_barrier_semaphore()
    for dev in [xdev(i) for i in xpeers] + [wdev(i) for i in wpeers] + [zdev(i) for i in zpeers]:
        pl.semaphore_signal(barrier, inc=1, device_id=dev, device_id_type=MESH)

    def entered():
        pl.semaphore_wait(barrier, NX + NW + NZ - 3)

    t0, t1 = transfer_ref[0:1, :], transfer_ref[1:2, :]
    p0, p1 = pivot_ref[0:1, :], pivot_ref[1:2, :]
    for n, row in enumerate((t0, t1, p0, p1, t0, t1, p0, p1)):
        coef[x, n : n + 1] = row

    def coefficients_first():
        for i in xpeers:
            send(coef.at[x], coef.at[x], k_send.at[2, 0, i], k_recv.at[2, 0, x], xdev(i))

    def coefficients_second():
        for i in xpeers:
            arrive(coef.at[i], k_send.at[2, 0, i], k_recv.at[2, 0, i], xdev(i))

    def rates_first():
        rate_group[w] = jnp.broadcast_to(t0 * t1, (8, dofs))
        for i in wpeers:
            send(rate_group.at[w], rate_group.at[w], r_send.at[0, i], r_recv.at[0, w], wdev(i))

    def rates_second():
        for i in wpeers:
            arrive(rate_group.at[i], r_send.at[0, i], r_recv.at[0, i], wdev(i))
        total = rate_group[0]
        for i in range(1, NW):
            total = total * rate_group[i]
        rate_zone[z] = total
        for i in zpeers:
            send(rate_zone.at[z], rate_zone.at[z], r_send.at[1, i], r_recv.at[1, z], zdev(i))

    def rates_third():
        for i in zpeers:
            arrive(rate_zone.at[i], r_send.at[1, i], r_recv.at[1, i], zdev(i))

    def build_incidence():
        sensors = pairs_ref.shape[2]
        for s in range(2):
            upper = pairs_ref[s, 0:1, :] - x * dofs
            lower = pairs_ref[s, 1:2, :] - x * dofs
            for b in range(0, dofs, 128):
                ids = lax.broadcasted_iota(jnp.int32, (128, sensors), 0) + b
                e = jnp.where(ids == upper, 1.0, 0.0) - jnp.where(ids == lower, 1.0, 0.0)
                E[s, b : b + 128] = e.astype(BF16)

    def project(v, k, j):
        t = targets[j]
        if v == 0:
            if j in a_copies:
                a_copies.pop(j).wait()
            val = jnp.concatenate([load_ref[s * cols + k * hc : s * cols + (k + 1) * hc, :] for s in range(2)], axis=0)
            part[k, j] = mm(val, A[block(t), :], NT)
        else:
            part[k, j] = mm(adj[k], S[:, block(t)], NN)

    def term(v, k, q, j, lo=0, n=hc):
        low = part[k, j, lo : lo + n]
        high = part[k, j, hc + lo : hc + lo + n]
        if v == 0:
            return high if q == 1 else low
        return high if q == 1 else low + high * coef[targets[j], 1:2, :]

    def rs_opp(v, k, q):
        for n, dev in ((0, right), (1, left)):
            opp_out[v, k, q, n] = term(v, k, q, 0, n * half, half).astype(BF16)
            send(
                opp_out.at[v, k, q, n], opp_in.at[v, k, q, n],
                x_send.at[v, k, q, n], x_recv.at[v, k, q, n], xdev(dev),
            )

    def rs_mid(v, k, q):
        for n, dev, back in ((0, right, left), (1, left, right)):
            arrive(opp_in.at[v, k, q, n], x_send.at[v, k, q, n], x_recv.at[v, k, q, n], xdev(back))
            own, other = n * half, (1 - n) * half
            mine = term(v, k, q, 1 + n, own, half) + opp_in[v, k, q, n].astype(F32)
            mid_out[v, k, q, n, own : own + half] = mine.astype(BF16)
            mid_out[v, k, q, n, other : other + half] = term(v, k, q, 1 + n, other, half).astype(BF16)
            send(
                mid_out.at[v, k, q, n], mid_in.at[v, k, q, n],
                x_send.at[v, k, q, 2 + n], x_recv.at[v, k, q, 2 + n], xdev(dev),
            )

    def rs_end(v, k, q):
        for n, back in ((0, left), (1, right)):
            arrive(mid_in.at[v, k, q, n], x_send.at[v, k, q, 2 + n], x_recv.at[v, k, q, 2 + n], xdev(back))
        total = term(v, k, q, 3) + mid_in[v, k, q, 0].astype(F32) + mid_in[v, k, q, 1].astype(F32)
        if v == 0:
            if q == 0:
                keep[k] = total * p0
            else:
                total = total * p1
                scan_first(v, k, keep[k] * t1 + total)
                early_first(v, k, total)
        else:
            if q == 0:
                keep[k] = total
                scan_first(v, k, total * t0)
            else:
                early_first(v, k, keep[k] - total * t1)
                keep[k] = total

    def early_first(v, k, val):
        early[v, k] = val.astype(BF16)
        for n, dev in ((0, right), (1, left)):
            send(early.at[v, k], early_in.at[v, k, n], x_send.at[v, k, n, 4], x_recv.at[v, k, n, 4], xdev(dev))

    def early_second(v, k):
        for n, dev, back in ((0, right, left), (1, left, right)):
            arrive(early_in.at[v, k, n], x_send.at[v, k, n, 4], x_recv.at[v, k, n, 4], xdev(back))
            at = pl.ds(n * half, half)
            send(
                early_in.at[v, k, n, at], early_in.at[v, k, 2, at],
                x_send.at[v, k, n, 5], x_recv.at[v, k, n, 5], xdev(dev),
            )

    def scan_first(v, k, val):
        val = val.astype(BF16)
        for h in range(2):
            shift[v, k, h * 4 : (h + 1) * 4] = val[:, h * hm : (h + 1) * hm].reshape(4, lane, hm)
        for i in wpeers:
            send(
                shift.at[v, k, i], group_in.at[v, k, w],
                c_send.at[v, k, 0, i], c_recv.at[v, k, 0, w], wdev(i),
            )
        group_in[v, k, w] = shift[v, k, w]

    def order(v, n):
        return range(n) if v == 0 else range(n - 1, -1, -1)

    def worker_lanes():
        return pl.ds(pl.multiple_of(lax.div(w, 4) * hm, 128), hm)

    def scan_second(v, k):
        for i in wpeers:
            arrive(group_in.at[v, k, i], c_send.at[v, k, 0, i], c_recv.at[v, k, 0, i], wdev(i))
        total = None
        for i in order(v, NW):
            new = group_in[v, k, i].astype(F32)
            total = new if total is None else total * rate_group[i, 0:1, worker_lanes()] + new
        zone_in[v, k, z] = total.astype(BF16)
        for i in zpeers:
            send(
                zone_in.at[v, k, z], zone_in.at[v, k, z],
                c_send.at[v, k, 1, i], c_recv.at[v, k, 1, z], zdev(i),
            )

    def scan_third(v, k):
        for i in zpeers:
            arrive(zone_in.at[v, k, i], c_send.at[v, k, 1, i], c_recv.at[v, k, 1, i], zdev(i))
        state = jnp.zeros((lane, hm), F32)
        for i in order(v, NZ):
            ahead = (i < z) if v == 0 else (i > z)
            new = state * rate_zone[i, 0:1, worker_lanes()] + zone_in[v, k, i].astype(F32)
            state = jnp.where(ahead, new, state)
        for i in order(v, NW):
            reply[v, k, i] = state.astype(BF16)
            state = state * rate_group[i, 0:1, worker_lanes()] + group_in[v, k, i].astype(F32)
        for i in wpeers:
            send(
                reply.at[v, k, i], car.at[v, k, w],
                c_send.at[v, k, 2, i], c_recv.at[v, k, 2, w], wdev(i),
            )
        car[v, k, w] = reply[v, k, w]

    def late_first(v, k):
        for i in wpeers:
            arrive(car.at[v, k, i], c_send.at[v, k, 2, i], c_recv.at[v, k, 2, i], wdev(i))
        for h in range(2):
            at = slice(h * hm, (h + 1) * hm)
            c = car[v, k, h * 4 : (h + 1) * 4].reshape(hc, hm).astype(F32)
            if v == 0:
                c = c * t0[:, at]
            late[v, k, :, at] = (keep[k, :, at] + c).astype(BF16)
        for n, dev in ((2, oppo), (0, right), (1, left)):
            send(late.at[v, k], late_in.at[v, k, n], k_send.at[v, k, n], k_recv.at[v, k, n], xdev(dev))

    def expand(v, k, n):
        t = (left, right, oppo, x)[n]
        if n == 3:
            last, first = late[v, k], early[v, k]
        else:
            if n == 2:
                for m, back in ((0, left), (1, right)):
                    at = pl.ds(m * half, half)
                    arrive(early_in.at[v, k, 2, at], x_send.at[v, k, m, 5], x_recv.at[v, k, m, 5], xdev(back))
            arrive(late_in.at[v, k, n], k_send.at[v, k, n], k_recv.at[v, k, n], xdev(t))
            last, first = late_in[v, k, n], early_in[v, k, n]
        grown = first.astype(F32) + last.astype(F32) * coef[t, 1:2, :]
        if v == 0:
            val = jnp.concatenate([last, grown.astype(BF16)], axis=0)
            new = mm(val, S[:, block(t)], NT)
        else:
            low = (grown * coef[t, 2:3, :]).astype(BF16)
            high = (last.astype(F32) * coef[t, 3:4, :]).astype(BF16)
            val = jnp.concatenate([low, high], axis=0)
            new = mm(val, A[block(t), :], NN)
        acc[k] = new if n == 3 else acc[k] + new

    def expand_own(v, k):
        if s_copies:
            s_copies.pop().wait()
        expand(v, k, 3)

    def expand_rest(v, k):
        for n in range(3):
            expand(v, k, n)

    quarter = 2 * hc // NX

    def sensors_first(k):
        for s in range(2):
            r = mm(acc[k, s * hc : (s + 1) * hc].astype(BF16), E[s], NN).astype(BF16)
            read_out[k, 2 * s : 2 * s + 2] = r.reshape(2, quarter, r.shape[-1])
        for i in xpeers:
            send(read_out.at[k, i], read_in.at[k, x], q_send.at[k, 0, i], q_recv.at[k, 0, x], xdev(i))
        read_in[k, x] = read_out[k, x]

    def sensors_second(k):
        for i in xpeers:
            arrive(read_in.at[k, i], q_send.at[k, 0, i], q_recv.at[k, 0, i], xdev(i))
        total = read_in[k, 0].astype(F32)
        for i in range(1, NX):
            total = total + read_in[k, i].astype(F32)
        weight = weights_ref[pl.ds(lax.div(x, 2), 1), :]
        wread[k, x] = (total * weight).astype(BF16)
        for i in xpeers:
            send(wread.at[k, x], wread.at[k, x], q_send.at[k, 1, i], q_recv.at[k, 1, x], xdev(i))

    def sensors_third(k):
        for i in xpeers:
            arrive(wread.at[k, i], q_send.at[k, 1, i], q_recv.at[k, 1, i], xdev(i))
        for s in range(2):
            r = wread[k, 2 * s : 2 * s + 2].reshape(hc, wread.shape[-1])
            adj[k, s * hc : (s + 1) * hc] = mm(r, E[s], NT).astype(BF16)

    def finish(k):
        for s in range(2):
            at = s * cols + k * hc
            out_ref[at : at + hc] = -disp_ref[s : s + 1, :] * acc[k, s * hc : (s + 1) * hc]

    steps = {
        "INC": build_incidence, "BAR": entered, "COEF1": coefficients_first, "COEF2": coefficients_second,
        "RATE1": rates_first, "RATE2": rates_second, "RATE3": rates_third,
        "P": project, "OPP": rs_opp, "MID": rs_mid, "END": rs_end, "AG2": early_second,
        "SC2": scan_second, "SC3": scan_third, "CAR": late_first, "EXP": expand_own, "EXQ": expand_rest,
        "SEN1": sensors_first, "SEN2": sensors_second, "ADJ": sensors_third, "OUT": finish,
    }
    for name in ORDER:
        if name in steps:
            steps[name]()
            continue
        stem = name[:1] if name[0] == "P" else name[:4] if name[:3] == "SEN" else name[:3]
        steps[stem](*(int(d) for d in name[len(stem) :]))
    for c in pending:
        c.wait_send()


def chain(load, pivot, transfer, disp, pairs, weights, analysis, synthesis):
    rows, dofs = load.shape
    modes = analysis.shape[0]
    cols = rows // 2
    sensors = pairs.shape[2]
    vm = pltpu.VMEM
    dma = pltpu.SemaphoreType.DMA
    hc = cols // NU
    hm = dofs // 2
    lane = 2 * hc // NW
    scratch = [
        vm((modes, dofs), BF16),
        vm((dofs, modes), BF16),
        vm((2, dofs, sensors), BF16),
        vm((NU, 2 * hc, dofs), F32),
        vm((NU, 4, 2 * hc, dofs), F32),
        vm((NU, hc, dofs), F32),
        vm((2, NU, 2, 2, hc // 2, dofs), BF16),
        vm((2, NU, 2, 2, hc // 2, dofs), BF16),
        vm((2, NU, 2, 2, hc, dofs), BF16),
        vm((2, NU, 2, 2, hc, dofs), BF16),
        vm((2, NU, hc, dofs), BF16),
        vm((2, NU, 3, hc, dofs), BF16),
        vm((2, NU, hc, dofs), BF16),
        vm((2, NU, 3, hc, dofs), BF16),
        vm((2, NU, NW, lane, hm), BF16),
        vm((2, NU, NW, lane, hm), BF16),
        vm((2, NU, NZ, lane, hm), BF16),
        vm((2, NU, NW, lane, hm), BF16),
        vm((2, NU, NW, lane, hm), BF16),
        vm((NX, 8, dofs), F32),
        vm((NW, 8, dofs), F32),
        vm((NZ, 8, dofs), F32),
        vm((NU, NX, 2 * hc // NX, sensors), BF16),
        vm((NU, NX, 2 * hc // NX, sensors), BF16),
        vm((NU, NX, 2 * hc // NX, sensors), BF16),
        vm((NU, 2 * hc, dofs), BF16),
        dma((4,)), dma((1,)),
        dma((2, NU, 2, 6)), dma((2, NU, 2, 6)),
        dma((3, NU, 4)), dma((3, NU, 4)),
        dma((2, NU, 3, 8)), dma((2, NU, 3, 8)),
        dma((2, 8)), dma((2, 8)),
        dma((NU, 2, 4)), dma((NU, 2, 4)),
    ]
    in_vmem = pl.BlockSpec(memory_space=pltpu.VMEM)
    in_hbm = pl.BlockSpec(memory_space=pl.ANY)
    return pl.pallas_call(
        kernel,
        out_shape=jax.ShapeDtypeStruct((rows, dofs), F32),
        in_specs=[in_vmem] * 6 + [in_hbm] * 2,
        out_specs=in_vmem,
        scratch_shapes=scratch,
        compiler_params=pltpu.CompilerParams(
            collective_id=0, has_side_effects=True, vmem_limit_bytes=56 * 1024 * 1024
        ),
        cost_estimate=pl.CostEstimate(
            flops=8 * rows * modes * dofs, bytes_accessed=4 * modes * dofs, transcendentals=0
        ),
        name="chain",
    )(load, pivot, transfer, disp, pairs, weights, analysis, synthesis)


def local(synthesis, analysis, pivot, transfer, displacement, directions, sensor_pairs, sensor_weights):
    dofs, storeys, columns = directions.shape
    load = (-(displacement.T[:, :, None] * directions.astype(F32))).astype(BF16)
    load = load.transpose(1, 2, 0).reshape(storeys * columns, dofs)
    pairs = sensor_pairs.transpose(0, 2, 1)
    out = chain(load, pivot, transfer, displacement, pairs, sensor_weights, analysis, synthesis)
    return out.reshape(storeys, columns, dofs).transpose(2, 0, 1)


def solution(mesh):
    return jax.shard_map(
        local,
        mesh=mesh,
        in_specs=(
            P("inner", None),
            P(None, "inner"),
            P("storey", "inner"),
            P("storey", "inner"),
            P("storey", "inner"),
            P("inner", "storey", None),
            P("storey", None, None),
            P("storey", None),
        ),
        out_specs=P("inner", "storey", None),
        check_vma=False,
    )
```

time: 109 us -> 104 us (0.954); the launches traced: 107 us -> 104 us
  Pallas kernels: 101 us -> 98.1 us
    pallas_call x1, Pallas kernels: 101 us -> 98.1 us  [chain(): pl.pallas_call(kernel, out_shape=jax.ShapeDtypeStruct((rows, dofs), F32),...]
where the time goes in v3:
time: 104 us
  Pallas kernels  98.1 us (94%)
  local copies, waits for them, and re-layouts  4.01 us (4%)
  other arithmetic  1.91 us (2%)
    pallas_call x1, Pallas kernels, chain(): pl.pallas_call(kernel, out_shape=jax.ShapeDtypeStruct((rows, dofs), F32),...  98.1 us
    reshape x1, local copies, waits for them, and re-layouts, local(): return out.reshape(storeys, columns, dofs).transpose(2, 0, 1)  2.09 us

profile of v3, /device:TPU:1, one launch (start us, length us, event | category | flops | bytes accessed | tf_op | source)
XLA Modules:
  0.0 104.0 jit_solution(7357782969272347868)
XLA Ops:
  0.0 0.9 copy.9
  0.9 1.9 %fusion = bf16[2,128,768]{1,0,2:T(2,128)(2,1)S(1)} fusion(bf16[768,2,128]{2,1,0:T(2,128)(2,1)} %param.13, f32[768,2]{1,0:T(8,128)S(1)} %copy.9), kind=kLoop, calls=%fused_computation.1 | loop fusion | flops 786432 | bytes 792576 | tf_op jit(solution)/shard_map/transpose | solution.py:422
  2.8 1.0 %copy.10 = bf16[2,128,768]{2,1,0:T(8,128)(2,1)} copy(bf16[2,128,768]{1,0,2:T(2,128)(2,1)S(1)} %fusion) | data formatting | bytes 786432 | tf_op jit(solution)/shard_map/transpose | solution.py:422
  3.8 98.1 %chain.1 = f32[256,768]{1,0:T(8,128)} custom-call(bf16[256,768]{1,0:T(8,128)(2,1)} %bitcast.8, f32[2,768]{1,0:T(2,128)} %pivot_ref.1, f32[2,768]{1,0:T(2,128)} %transfer_ref.1, f32[2,768]{1,0:T(2,128)} %disp_ref.1, s32[2,2,512]{2,1,0:T(2,128)} %bitcast.10, f32[2,512]{1,0:T(2,128)} %weights_ref.1, bf16[3072,768]{1,0:T(8,128)(2,1)} %analysis_hbm.1, ...), custom_call_target="tpu_custom_call" | custom-call | flops 4831838208 | bytes 9437184 | tf_op jit(solution)/shard_map/chain/pallas_call | solution.py:403
  101.9 2.1 %copy.11 = f32[2,128,768]{1,0,2:T(2,128)} copy(f32[2,128,768]{2,1,0:T(8,128)} %bitcast.7) | data formatting | bytes 1572864 | tf_op jit(solution)/shard_map/reshape | solution.py:425

commit v4 on v3

--- a/solution.py
+++ b/solution.py
@@ -18,12 +18,12 @@
 NT = (((1,), (1,)), ((), ()))
 
 ORDER = (
-    "INC", "P002", "P001", "BAR", "COEF1", "RATE1", "P000", "OPP000", "OPP001", "P003", "P013", "P010", "OPP010",
-    "OPP011", "P012", "P011", "COEF2", "RATE2", "MID000", "MID001", "MID010", "MID011", "END000", "RATE3", "END001",
+    "P000", "BAR", "OPP000", "COEF1", "OPP001", "P013", "P003", "RATE1", "P001", "P002", "P011", "P010", "OPP010",
+    "OPP011", "INC", "P012", "MID000", "COEF2", "RATE2", "MID001", "MID010", "MID011", "END000", "RATE3", "END001",
     "END010", "END011", "SC200", "AG200", "SC201", "AG201", "SC300", "SC301", "CAR00", "EXP00", "CAR01", "EXP01",
-    "EXQ00", "SEN10", "EXQ01", "SEN11", "SEN20", "SEN21", "ADJ0", "P100", "OPP100", "P102", "P103", "P101",
-    "OPP101", "ADJ1", "P110", "OPP110", "MID100", "P111", "P112", "OPP111", "P113", "MID101", "MID110", "END100",
-    "MID111", "END101", "SC210", "END110", "END111", "AG210", "SC211", "SC310", "AG211", "CAR10", "SC311", "EXP10",
+    "EXQ00", "SEN10", "EXQ01", "SEN11", "SEN20", "SEN21", "ADJ0", "P101", "P100", "OPP100", "OPP101", "P102",
+    "P103", "ADJ1", "P110", "OPP110", "P113", "OPP111", "P111", "P112", "MID100", "MID101", "MID110", "MID111",
+    "END100", "END101", "END110", "SC210", "END111", "AG210", "SC211", "SC310", "AG211", "SC311", "CAR10", "EXP10",
     "CAR11", "EXP11", "EXQ10", "OUT0", "EXQ11", "OUT1",
 )
 
@@ -33,19 +33,20 @@
 
 
 def kernel(
-    load_ref, pivot_ref, transfer_ref, disp_ref, pairs_ref, weights_ref, analysis_hbm, synthesis_hbm,
+    directions_hbm, pivot_hbm, transfer_hbm, disp_hbm, pairs_hbm, weights_hbm, analysis_hbm, synthesis_hbm,
     out_ref,
+    directions_ref, pivot_ref, transfer_ref, disp_ref, pairs_ref, weights_ref, load_ref,
     A, S, E, acc, part, keep, opp_out, opp_in, mid_out, mid_in, early, early_in, late, late_in,
     shift, group_in, zone_in, reply, car, coef, rate_group, rate_zone,
     read_out, read_in, wread, adj,
-    a_sem, s_sem, x_send, x_recv, k_send, k_recv, c_send, c_recv, r_send, r_recv, q_send, q_recv,
+    in_sem, a_sem, s_sem, x_send, x_recv, k_send, k_recv, c_send, c_recv, r_send, r_recv, q_send, q_recv,
 ):
     storey = lax.axis_index("storey")
     x = lax.axis_index("inner")
     z = lax.div(storey, NW)
     w = lax.rem(storey, NW)
-    rows, dofs = load_ref.shape
-    cols = rows // 2
+    dofs, _, cols = directions_ref.shape
+    rows = 2 * cols
     hc = cols // NU
     half = hc // 2
     lane = 2 * hc // NW
@@ -83,22 +84,36 @@
     def block(t):
         return pl.ds(pl.multiple_of(t * dofs, 128), dofs)
 
-    targets = (oppo, right, left, x)
-    a_copies = {}
-    for j in (0, 1, 2, 3):
-        at = block(targets[j])
-        c = pltpu.make_async_copy(analysis_hbm.at[at, :], A.at[at, :], a_sem.at[j])
-        c.start()
-        a_copies[j] = c
-    s_copies = [pltpu.make_async_copy(synthesis_hbm, S, s_sem.at[0])]
-    s_copies[0].start()
-
     barrier = pltpu.get_barrier_semaphore()
-    for dev in [xdev(i) for i in xpeers] + [wdev(i) for i in wpeers] + [zdev(i) for i in zpeers]:
+    for dev in [zdev(i) for i in zpeers] + [wdev(i) for i in wpeers] + [xdev(i) for i in xpeers]:
         pl.semaphore_signal(barrier, inc=1, device_id=dev, device_id_type=MESH)
 
     def entered():
         pl.semaphore_wait(barrier, NX + NW + NZ - 3)
+
+    def fetch(src, dst, sem):
+        c = pltpu.make_async_copy(src, dst, sem)
+        c.start()
+        return c
+
+    targets = (oppo, right, left, x)
+    small = [fetch(directions_hbm, directions_ref, in_sem.at[0]), fetch(disp_hbm, disp_ref, in_sem.at[1])]
+    a_copies = {0: fetch(analysis_hbm.at[block(targets[0]), :], A.at[block(targets[0]), :], a_sem.at[0])}
+    others = ((pivot_hbm, pivot_ref), (transfer_hbm, transfer_ref), (pairs_hbm, pairs_ref), (weights_hbm, weights_ref))
+    more = [fetch(src, dst, in_sem.at[2 + n]) for n, (src, dst) in enumerate(others)]
+    for j in (1, 2, 3):
+        a_copies[j] = fetch(analysis_hbm.at[block(targets[j]), :], A.at[block(targets[j]), :], a_sem.at[j])
+    s_copies = [fetch(synthesis_hbm, S, s_sem.at[0])]
+
+    for c in small:
+        c.wait()
+    for b in range(0, dofs, 128):
+        both = directions_ref[b : b + 128].astype(F32)
+        for s in range(2):
+            turned = jnp.transpose(both[:, s, :], (1, 0))
+            load_ref[s * cols : (s + 1) * cols, b : b + 128] = (-disp_ref[s : s + 1, b : b + 128] * turned).astype(BF16)
+    for c in more:
+        c.wait()
 
     t0, t1 = transfer_ref[0:1, :], transfer_ref[1:2, :]
     p0, p1 = pivot_ref[0:1, :], pivot_ref[1:2, :]
@@ -354,17 +369,19 @@
         c.wait_send()
 
 
-def chain(load, pivot, transfer, disp, pairs, weights, analysis, synthesis):
-    rows, dofs = load.shape
+def chain(directions, pivot, transfer, disp, pairs, weights, analysis, synthesis):
+    dofs, _, cols = directions.shape
+    rows = 2 * cols
     modes = analysis.shape[0]
-    cols = rows // 2
     sensors = pairs.shape[2]
     vm = pltpu.VMEM
     dma = pltpu.SemaphoreType.DMA
     hc = cols // NU
     hm = dofs // 2
     lane = 2 * hc // NW
-    scratch = [
+    small = (directions, pivot, transfer, disp, pairs, weights)
+    scratch = [vm(a.shape, a.dtype) for a in small] + [
+        vm((rows, dofs), BF16),
         vm((modes, dofs), BF16),
         vm((dofs, modes), BF16),
         vm((2, dofs, sensors), BF16),
@@ -391,7 +408,7 @@
         vm((NU, NX, 2 * hc // NX, sensors), BF16),
         vm((NU, NX, 2 * hc // NX, sensors), BF16),
         vm((NU, 2 * hc, dofs), BF16),
-        dma((4,)), dma((1,)),
+        dma((6,)), dma((4,)), dma((1,)),
         dma((2, NU, 2, 6)), dma((2, NU, 2, 6)),
         dma((3, NU, 4)), dma((3, NU, 4)),
         dma((2, NU, 3, 8)), dma((2, NU, 3, 8)),
@@ -403,7 +420,7 @@
     return pl.pallas_call(
         kernel,
         out_shape=jax.ShapeDtypeStruct((rows, dofs), F32),
-        in_specs=[in_vmem] * 6 + [in_hbm] * 2,
+        in_specs=[in_hbm] * 8,
         out_specs=in_vmem,
         scratch_shapes=scratch,
         compiler_params=pltpu.CompilerParams(
@@ -413,15 +430,13 @@
             flops=8 * rows * modes * dofs, bytes_accessed=4 * modes * dofs, transcendentals=0
         ),
         name="chain",
-    )(load, pivot, transfer, disp, pairs, weights, analysis, synthesis)
+    )(directions, pivot, transfer, disp, pairs, weights, analysis, synthesis)
 
 
 def local(synthesis, analysis, pivot, transfer, displacement, directions, sensor_pairs, sensor_weights):
     dofs, storeys, columns = directions.shape
-    load = (-(displacement.T[:, :, None] * directions.astype(F32))).astype(BF16)
-    load = load.transpose(1, 2, 0).reshape(storeys * columns, dofs)
     pairs = sensor_pairs.transpose(0, 2, 1)
-    out = chain(load, pivot, transfer, displacement, pairs, sensor_weights, analysis, synthesis)
+    out = chain(directions, pivot, transfer, displacement, pairs, sensor_weights, analysis, synthesis)
     return out.reshape(storeys, columns, dofs).transpose(2, 0, 1)
 
 

time: 104 us -> 98.4 us (0.946)
  local copies, waits for them, and re-layouts: 4.01 us -> 2.09 us
  other arithmetic: 1.91 us -> 0 us
  Pallas kernels: 98.1 us -> 96.2 us
    transpose x2 -> x0, local copies, waits for them, and re-layouts: 1.92 us -> none  [the longest x1 1.05 us: local(): load = load.transpose(1, 2, 0).reshape(storeys * columns, dofs)]
    transpose x1 -> x0, other arithmetic: 1.91 us -> none  [local(): load = load.transpose(1, 2, 0).reshape(storeys * columns, dofs)]
    pallas_call x1, Pallas kernels: 98.1 us -> 96.2 us  [chain(): pl.pallas_call(kernel, out_shape=jax.ShapeDtypeStruct((rows, dofs), F32),...]
where the time goes in v4:
time: 98.4 us; the launch traced here: 98.3 us
  Pallas kernels  96.2 us (98%)
  local copies, waits for them, and re-layouts  2.09 us (2%)
    pallas_call x1, Pallas kernels, chain(): pl.pallas_call(kernel, out_shape=jax.ShapeDtypeStruct((rows, dofs), F32),...  96.2 us
    reshape x1, local copies, waits for them, and re-layouts, local(): return out.reshape(storeys, columns, dofs).transpose(2, 0, 1)  2.09 us

profile of v4, /device:TPU:1, one launch (start us, length us, event | category | flops | bytes accessed | tf_op | source)
XLA Modules:
  0.0 98.3 jit_solution(18321640082381927105)
XLA Ops:
  0.0 96.2 %chain.1 = f32[256,768]{1,0:T(8,128)} custom-call(bf16[768,2,128]{2,1,0:T(2,128)(2,1)} %directions_hbm.1, f32[2,768]{1,0:T(2,128)} %pivot_hbm.1, f32[2,768]{1,0:T(2,128)} %transfer_hbm.1, f32[2,768]{1,0:T(2,128)} %disp_hbm.1, s32[2,2,512]{2,1,0:T(2,128)} %bitcast.4, f32[2,512]{1,0:T(2,128)} %weights_hbm.1, bf16[3072,768]{1,0:T(8,128)(2,1)} %analysis_hbm.1, ...), custom_call_target="tpu_custom_call" | custom-call | flops 4831838208 | bytes 9437184 | tf_op jit(solution)/shard_map/chain/pallas_call | solution.py:420
  96.2 2.1 %copy.9 = f32[2,128,768]{1,0,2:T(2,128)} copy(f32[2,128,768]{2,1,0:T(8,128)} %bitcast.3) | data formatting | bytes 1572864 | tf_op jit(solution)/shard_map/reshape | solution.py:440

commit v5 on v4

--- a/solution.py
+++ b/solution.py
@@ -18,13 +18,14 @@
 NT = (((1,), (1,)), ((), ()))
 
 ORDER = (
-    "P000", "BAR", "OPP000", "COEF1", "OPP001", "P013", "P003", "RATE1", "P001", "P002", "P011", "P010", "OPP010",
-    "OPP011", "INC", "P012", "MID000", "COEF2", "RATE2", "MID001", "MID010", "MID011", "END000", "RATE3", "END001",
-    "END010", "END011", "SC200", "AG200", "SC201", "AG201", "SC300", "SC301", "CAR00", "EXP00", "CAR01", "EXP01",
-    "EXQ00", "SEN10", "EXQ01", "SEN11", "SEN20", "SEN21", "ADJ0", "P101", "P100", "OPP100", "OPP101", "P102",
-    "P103", "ADJ1", "P110", "OPP110", "P113", "OPP111", "P111", "P112", "MID100", "MID101", "MID110", "MID111",
-    "END100", "END101", "END110", "SC210", "END111", "AG210", "SC211", "SC310", "AG211", "SC311", "CAR10", "EXP10",
-    "CAR11", "EXP11", "EXQ10", "OUT0", "EXQ11", "OUT1",
+    "BAR", "COEF1", "P000", "OPP000", "P012", "Z0", "P003", "OPP001", "P010", "OPP011", "OPP010", "P001", "P002",
+    "RATE1", "Z1", "P013", "P011", "INC", "COEF2", "Z2", "MID000", "MID001", "Z3", "RATE2", "MID011", "MID010",
+    "END000", "END001", "RATE3", "END010", "SC200", "END011", "AG200", "SC201", "AG201", "CAR00", "CAR01", "EXP00",
+    "EXQ001", "EXQ002", "EXQ000", "SEN10", "EXP01", "EXQ011", "EXQ010", "EXQ012", "SEN11", "SEN20", "SEN21", "ADJ0",
+    "P100", "OPP100", "P101", "P102", "P103", "OPP101", "ADJ1", "P110", "OPP110", "P113", "P112", "MID100",
+    "OPP111", "P111", "MID101", "MID110", "END100", "MID111", "END101", "SC210", "END110", "END111", "AG210",
+    "SC211", "CAR10", "AG211", "CAR11", "EXP10", "EXQ102", "EXQ100", "EXQ101", "OUT0", "EXP11", "EXQ111", "EXQ112",
+    "EXQ110", "OUT1",
 )
 
 
@@ -36,10 +37,11 @@
     directions_hbm, pivot_hbm, transfer_hbm, disp_hbm, pairs_hbm, weights_hbm, analysis_hbm, synthesis_hbm,
     out_ref,
     directions_ref, pivot_ref, transfer_ref, disp_ref, pairs_ref, weights_ref, load_ref,
-    A, S, E, acc, part, keep, opp_out, opp_in, mid_out, mid_in, early, early_in, late, late_in,
-    shift, group_in, zone_in, reply, car, coef, rate_group, rate_zone,
+    A, S, E, acc, part, keep, opp_out, opp_in, mid_out, mid_in, early, early_in, late_in,
+    shift, group_in, base, base_in, zone_in, reply, coef, rate_group, rate_zone,
     read_out, read_in, wread, adj,
-    in_sem, a_sem, s_sem, x_send, x_recv, k_send, k_recv, c_send, c_recv, r_send, r_recv, q_send, q_recv,
+    z_sem, in_sem, a_sem, s_sem, x_send, x_recv, k_send, k_recv, l_send, l_recv, a_recv,
+    c_send, c_recv, r_send, r_recv, q_send, q_recv,
 ):
     storey = lax.axis_index("storey")
     x = lax.axis_index("inner")
@@ -85,11 +87,19 @@
         return pl.ds(pl.multiple_of(t * dofs, 128), dofs)
 
     barrier = pltpu.get_barrier_semaphore()
-    for dev in [zdev(i) for i in zpeers] + [wdev(i) for i in wpeers] + [xdev(i) for i in xpeers]:
+    znext = (lax.rem(z + 1, NZ), lax.rem(z + NZ - 1, NZ))
+    for dev in [xdev(i) for i in xpeers] + [wdev(i) for i in wpeers] + [zdev(i) for i in znext]:
         pl.semaphore_signal(barrier, inc=1, device_id=dev, device_id_type=MESH)
 
     def entered():
-        pl.semaphore_wait(barrier, NX + NW + NZ - 3)
+        pl.semaphore_wait(barrier, NX + NW)
+
+    def along(r):
+        for n in range(2):
+            if r > 0:
+                pl.semaphore_wait(z_sem.at[r - 1, n], 1)
+            if r < 3:
+                pl.semaphore_signal(z_sem.at[r, n], inc=1, device_id=zdev(znext[n]), device_id_type=MESH)
 
     def fetch(src, dst, sem):
         c = pltpu.make_async_copy(src, dst, sem)
@@ -122,14 +132,16 @@
 
     def coefficients_first():
         for i in xpeers:
-            send(coef.at[x], coef.at[x], k_send.at[2, 0, i], k_recv.at[2, 0, x], xdev(i))
+            send(coef.at[x], coef.at[x], k_send.at[i], k_recv.at[x], xdev(i))
 
     def coefficients_second():
         for i in xpeers:
-            arrive(coef.at[i], k_send.at[2, 0, i], k_recv.at[2, 0, i], xdev(i))
+            arrive(coef.at[i], k_send.at[i], k_recv.at[i], xdev(i))
 
     def rates_first():
-        rate_group[w] = jnp.broadcast_to(t0 * t1, (8, dofs))
+        rate_group[w, 0:1] = t0 * t1
+        rate_group[w, 1:2] = t0
+        rate_group[w, 2:8] = jnp.broadcast_to(t0, (6, dofs))
         for i in wpeers:
             send(rate_group.at[w], rate_group.at[w], r_send.at[0, i], r_recv.at[0, w], wdev(i))
 
@@ -204,14 +216,15 @@
             else:
                 total = total * p1
                 scan_first(v, k, keep[k] * t1 + total)
+                to_workers(v, k, 2, base, base_in, keep[k])
                 early_first(v, k, total)
         else:
             if q == 0:
                 keep[k] = total
                 scan_first(v, k, total * t0)
             else:
+                to_workers(v, k, 2, base, base_in, total)
                 early_first(v, k, keep[k] - total * t1)
-                keep[k] = total
 
     def early_first(v, k, val):
         early[v, k] = val.astype(BF16)
@@ -227,16 +240,19 @@
                 x_send.at[v, k, n, 5], x_recv.at[v, k, n, 5], xdev(dev),
             )
 
-    def scan_first(v, k, val):
+    def to_workers(v, k, stage, out, into, val):
         val = val.astype(BF16)
         for h in range(2):
-            shift[v, k, h * 4 : (h + 1) * 4] = val[:, h * hm : (h + 1) * hm].reshape(4, lane, hm)
-        for i in wpeers:
-            send(
-                shift.at[v, k, i], group_in.at[v, k, w],
-                c_send.at[v, k, 0, i], c_recv.at[v, k, 0, w], wdev(i),
-            )
-        group_in[v, k, w] = shift[v, k, w]
+            out[v, k, h * 4 : (h + 1) * 4] = val[:, h * hm : (h + 1) * hm].reshape(4, lane, hm)
+        for i in wpeers:
+            send(
+                out.at[v, k, i], into.at[v, k, w],
+                c_send.at[v, k, stage, i], c_recv.at[v, k, stage, w], wdev(i),
+            )
+        into[v, k, w] = out[v, k, w]
+
+    def scan_first(v, k, val):
+        to_workers(v, k, 0, shift, group_in, val)
 
     def order(v, n):
         return range(n) if v == 0 else range(n - 1, -1, -1)
@@ -261,44 +277,44 @@
     def scan_third(v, k):
         for i in zpeers:
             arrive(zone_in.at[v, k, i], c_send.at[v, k, 1, i], c_recv.at[v, k, 1, i], zdev(i))
+        for i in wpeers:
+            arrive(base_in.at[v, k, i], c_send.at[v, k, 2, i], c_recv.at[v, k, 2, i], wdev(i))
         state = jnp.zeros((lane, hm), F32)
         for i in order(v, NZ):
             ahead = (i < z) if v == 0 else (i > z)
             new = state * rate_zone[i, 0:1, worker_lanes()] + zone_in[v, k, i].astype(F32)
             state = jnp.where(ahead, new, state)
         for i in order(v, NW):
-            reply[v, k, i] = state.astype(BF16)
+            grown = state * rate_group[i, 1:2, worker_lanes()] if v == 0 else state
+            reply[v, k, i] = (base_in[v, k, i].astype(F32) + grown).astype(BF16)
             state = state * rate_group[i, 0:1, worker_lanes()] + group_in[v, k, i].astype(F32)
         for i in wpeers:
             send(
-                reply.at[v, k, i], car.at[v, k, w],
-                c_send.at[v, k, 2, i], c_recv.at[v, k, 2, w], wdev(i),
-            )
-        car[v, k, w] = reply[v, k, w]
-
-    def late_first(v, k):
-        for i in wpeers:
-            arrive(car.at[v, k, i], c_send.at[v, k, 2, i], c_recv.at[v, k, 2, i], wdev(i))
-        for h in range(2):
-            at = slice(h * hm, (h + 1) * hm)
-            c = car[v, k, h * 4 : (h + 1) * 4].reshape(hc, hm).astype(F32)
-            if v == 0:
-                c = c * t0[:, at]
-            late[v, k, :, at] = (keep[k, :, at] + c).astype(BF16)
-        for n, dev in ((2, oppo), (0, right), (1, left)):
-            send(late.at[v, k], late_in.at[v, k, n], k_send.at[v, k, n], k_recv.at[v, k, n], xdev(dev))
+                reply.at[v, k, i], late_in.at[v, k, x, w],
+                l_send.at[v, k, 0, i], l_recv.at[v, k, 0, w], wdev(i),
+            )
+        for d, t in enumerate(xpeers):
+            for i in [w] + wpeers:
+                send(
+                    reply.at[v, k, i], late_in.at[v, k, x, w],
+                    l_send.at[v, k, 1 + d, i], a_recv.at[v, k, x], (z * NW + i, t),
+                )
+        late_in[v, k, x, w] = reply[v, k, w]
 
     def expand(v, k, n):
         t = (left, right, oppo, x)[n]
         if n == 3:
-            last, first = late[v, k], early[v, k]
+            for i in wpeers:
+                arrive(late_in.at[v, k, x, i], l_send.at[v, k, 0, i], l_recv.at[v, k, 0, i], wdev(i))
+            first = early[v, k]
         else:
             if n == 2:
                 for m, back in ((0, left), (1, right)):
                     at = pl.ds(m * half, half)
                     arrive(early_in.at[v, k, 2, at], x_send.at[v, k, m, 5], x_recv.at[v, k, m, 5], xdev(back))
-            arrive(late_in.at[v, k, n], k_send.at[v, k, n], k_recv.at[v, k, n], xdev(t))
-            last, first = late_in[v, k, n], early_in[v, k, n]
+            arrive(late_in.at[v, k, t], l_send.at[v, k, 1, 0], a_recv.at[v, k, t], xdev(t))
+            first = early_in[v, k, n]
+        last = jnp.concatenate([late_in[v, k, t, h * 4 : (h + 1) * 4].reshape(hc, hm) for h in range(2)], axis=1)
         grown = first.astype(F32) + last.astype(F32) * coef[t, 1:2, :]
         if v == 0:
             val = jnp.concatenate([last, grown.astype(BF16)], axis=0)
@@ -315,10 +331,6 @@
             s_copies.pop().wait()
         expand(v, k, 3)
 
-    def expand_rest(v, k):
-        for n in range(3):
-            expand(v, k, n)
-
     quarter = 2 * hc // NX
 
     def sensors_first(k):
@@ -353,17 +365,17 @@
             out_ref[at : at + hc] = -disp_ref[s : s + 1, :] * acc[k, s * hc : (s + 1) * hc]
 
     steps = {
-        "INC": build_incidence, "BAR": entered, "COEF1": coefficients_first, "COEF2": coefficients_second,
+        "INC": build_incidence, "BAR": entered, "Z": along, "COEF1": coefficients_first, "COEF2": coefficients_second,
         "RATE1": rates_first, "RATE2": rates_second, "RATE3": rates_third,
         "P": project, "OPP": rs_opp, "MID": rs_mid, "END": rs_end, "AG2": early_second,
-        "SC2": scan_second, "SC3": scan_third, "CAR": late_first, "EXP": expand_own, "EXQ": expand_rest,
+        "SC2": scan_second, "CAR": scan_third, "EXP": expand_own, "EXQ": expand,
         "SEN1": sensors_first, "SEN2": sensors_second, "ADJ": sensors_third, "OUT": finish,
     }
     for name in ORDER:
         if name in steps:
             steps[name]()
             continue
-        stem = name[:1] if name[0] == "P" else name[:4] if name[:3] == "SEN" else name[:3]
+        stem = name[:1] if name[0] in "PZ" else name[:4] if name[:3] == "SEN" else name[:3]
         steps[stem](*(int(d) for d in name[len(stem) :]))
     for c in pending:
         c.wait_send()
@@ -394,12 +406,12 @@
         vm((2, NU, 2, 2, hc, dofs), BF16),
         vm((2, NU, hc, dofs), BF16),
         vm((2, NU, 3, hc, dofs), BF16),
-        vm((2, NU, hc, dofs), BF16),
-        vm((2, NU, 3, hc, dofs), BF16),
+        vm((2, NU, NX, NW, lane, hm), BF16),
+        vm((2, NU, NW, lane, hm), BF16),
+        vm((2, NU, NW, lane, hm), BF16),
         vm((2, NU, NW, lane, hm), BF16),
         vm((2, NU, NW, lane, hm), BF16),
         vm((2, NU, NZ, lane, hm), BF16),
-        vm((2, NU, NW, lane, hm), BF16),
         vm((2, NU, NW, lane, hm), BF16),
         vm((NX, 8, dofs), F32),
         vm((NW, 8, dofs), F32),
@@ -408,9 +420,11 @@
         vm((NU, NX, 2 * hc // NX, sensors), BF16),
         vm((NU, NX, 2 * hc // NX, sensors), BF16),
         vm((NU, 2 * hc, dofs), BF16),
+        pltpu.SemaphoreType.REGULAR((3, 2)),
         dma((6,)), dma((4,)), dma((1,)),
         dma((2, NU, 2, 6)), dma((2, NU, 2, 6)),
-        dma((3, NU, 4)), dma((3, NU, 4)),
+        dma((NX,)), dma((NX,)),
+        dma((2, NU, NX, NW)), dma((2, NU, 1, NW)), dma((2, NU, NX)),
         dma((2, NU, 3, 8)), dma((2, NU, 3, 8)),
         dma((2, 8)), dma((2, 8)),
         dma((NU, 2, 4)), dma((NU, 2, 4)),

time: 98.4 us -> 92.1 us (0.936)
  Pallas kernels: 96.2 us -> 89.9 us
    pallas_call x1, Pallas kernels: 96.2 us -> 89.9 us  [chain(): pl.pallas_call(kernel, out_shape=jax.ShapeDtypeStruct((rows, dofs), F32),...]
where the time goes in v5:
time: 92.1 us; the launch traced here: 92 us
  Pallas kernels  89.9 us (98%)
  local copies, waits for them, and re-layouts  2.09 us (2%)
    pallas_call x1, Pallas kernels, chain(): pl.pallas_call(kernel, out_shape=jax.ShapeDtypeStruct((rows, dofs), F32),...  89.9 us
    reshape x1, local copies, waits for them, and re-layouts, local(): return out.reshape(storeys, columns, dofs).transpose(2, 0, 1)  2.09 us

profile of v5, /device:TPU:1, one launch (start us, length us, event | category | flops | bytes accessed | tf_op | source)
XLA Modules:
  0.0 92.0 jit_solution(11843682824656729129)
XLA Ops:
  0.0 89.9 %chain.1 = f32[256,768]{1,0:T(8,128)} custom-call(bf16[768,2,128]{2,1,0:T(2,128)(2,1)} %directions_hbm.1, f32[2,768]{1,0:T(2,128)} %pivot_hbm.1, f32[2,768]{1,0:T(2,128)} %transfer_hbm.1, f32[2,768]{1,0:T(2,128)} %disp_hbm.1, s32[2,2,512]{2,1,0:T(2,128)} %bitcast.4, f32[2,512]{1,0:T(2,128)} %weights_hbm.1, bf16[3072,768]{1,0:T(8,128)(2,1)} %analysis_hbm.1, ...), custom_call_target="tpu_custom_call" | custom-call | flops 4831838208 | bytes 9437184 | tf_op jit(solution)/shard_map/chain/pallas_call | solution.py:434
  89.9 2.1 %copy.9 = f32[2,128,768]{1,0,2:T(2,128)} copy(f32[2,128,768]{2,1,0:T(8,128)} %bitcast.3) | data formatting | bytes 1572864 | tf_op jit(solution)/shard_map/reshape | solution.py:454

commit v6 on v5

--- a/solution.py
+++ b/solution.py
@@ -20,12 +20,12 @@
 ORDER = (
     "BAR", "COEF1", "P000", "OPP000", "P012", "Z0", "P003", "OPP001", "P010", "OPP011", "OPP010", "P001", "P002",
     "RATE1", "Z1", "P013", "P011", "INC", "COEF2", "Z2", "MID000", "MID001", "Z3", "RATE2", "MID011", "MID010",
-    "END000", "END001", "RATE3", "END010", "SC200", "END011", "AG200", "SC201", "AG201", "CAR00", "CAR01", "EXP00",
-    "EXQ001", "EXQ002", "EXQ000", "SEN10", "EXP01", "EXQ011", "EXQ010", "EXQ012", "SEN11", "SEN20", "SEN21", "ADJ0",
-    "P100", "OPP100", "P101", "P102", "P103", "OPP101", "ADJ1", "P110", "OPP110", "P113", "P112", "MID100",
-    "OPP111", "P111", "MID101", "MID110", "END100", "MID111", "END101", "SC210", "END110", "END111", "AG210",
-    "SC211", "CAR10", "AG211", "CAR11", "EXP10", "EXQ102", "EXQ100", "EXQ101", "OUT0", "EXP11", "EXQ111", "EXQ112",
-    "EXQ110", "OUT1",
+    "END000", "END001", "RATE3", "END010", "SC200", "END011", "AG200", "SC201", "AG201", "CAR00", "CAR01", "FL80",
+    "EXP00", "EXQ001", "EXQ002", "EXQ000", "SEN10", "EXP01", "EXQ011", "EXQ010", "EXQ012", "SEN11", "SEN20",
+    "SEN21", "FL12", "ADJ0", "P100", "OPP100", "P101", "P102", "P103", "OPP101", "ADJ1", "P110", "OPP110", "P113",
+    "P112", "MID100", "OPP111", "P111", "MID101", "MID110", "END100", "MID111", "FL24", "END101", "SC210", "END110",
+    "END111", "AG210", "FL40", "SC211", "CAR10", "AG211", "CAR11", "FL66", "EXP10", "EXQ102", "EXQ100", "EXQ101",
+    "OUT0", "FL31", "EXP11", "EXQ111", "EXQ112", "EXQ110", "OUT1",
 )
 
 
@@ -75,11 +75,16 @@
         c.start()
         pending.append(c)
 
+    def flush(keep):
+        while len(pending) > keep:
+            pending.pop(0).wait_send()
+
     def arrive(dst, ssem, rsem, dev):
         remote(dst, dst, ssem, rsem, dev).wait_recv()
 
     def peers(me, n):
-        return [lax.rem(me + d, n) for d in range(1, n)]
+        far_first = sorted(range(1, n), key=lambda d: -min(d, n - d))
+        return [lax.rem(me + d, n) for d in far_first]
 
     xpeers, wpeers, zpeers = [oppo, right, left], peers(w, NW), peers(z, NZ)
 
@@ -216,15 +221,15 @@
             else:
                 total = total * p1
                 scan_first(v, k, keep[k] * t1 + total)
+                early_first(v, k, total)
                 to_workers(v, k, 2, base, base_in, keep[k])
-                early_first(v, k, total)
         else:
             if q == 0:
                 keep[k] = total
                 scan_first(v, k, total * t0)
             else:
+                early_first(v, k, keep[k] - total * t1)
                 to_workers(v, k, 2, base, base_in, total)
-                early_first(v, k, keep[k] - total * t1)
 
     def early_first(v, k, val):
         early[v, k] = val.astype(BF16)
@@ -288,17 +293,17 @@
             grown = state * rate_group[i, 1:2, worker_lanes()] if v == 0 else state
             reply[v, k, i] = (base_in[v, k, i].astype(F32) + grown).astype(BF16)
             state = state * rate_group[i, 0:1, worker_lanes()] + group_in[v, k, i].astype(F32)
-        for i in wpeers:
-            send(
-                reply.at[v, k, i], late_in.at[v, k, x, w],
-                l_send.at[v, k, 0, i], l_recv.at[v, k, 0, w], wdev(i),
-            )
         for d, t in enumerate(xpeers):
-            for i in [w] + wpeers:
+            for i in wpeers + [w]:
                 send(
                     reply.at[v, k, i], late_in.at[v, k, x, w],
                     l_send.at[v, k, 1 + d, i], a_recv.at[v, k, x], (z * NW + i, t),
                 )
+        for i in wpeers:
+            send(
+                reply.at[v, k, i], late_in.at[v, k, x, w],
+                l_send.at[v, k, 0, i], l_recv.at[v, k, 0, w], wdev(i),
+            )
         late_in[v, k, x, w] = reply[v, k, w]
 
     def expand(v, k, n):
@@ -375,10 +380,12 @@
         if name in steps:
             steps[name]()
             continue
+        if name[:2] == "FL":
+            flush(int(name[2:]))
+            continue
         stem = name[:1] if name[0] in "PZ" else name[:4] if name[:3] == "SEN" else name[:3]
         steps[stem](*(int(d) for d in name[len(stem) :]))
-    for c in pending:
-        c.wait_send()
+    flush(0)
 
 
 def chain(directions, pivot, transfer, disp, pairs, weights, analysis, synthesis):

time: 92.1 us -> 90.9 us (0.987)
  Pallas kernels: 89.9 us -> 88.7 us
    pallas_call x1, Pallas kernels: 89.9 us -> 88.7 us  [chain(): pl.pallas_call(kernel, out_shape=jax.ShapeDtypeStruct((rows, dofs), F32),...]
where the time goes in v6:
time: 90.9 us; the launch traced here: 90.8 us
  Pallas kernels  88.7 us (98%)
  local copies, waits for them, and re-layouts  2.09 us (2%)
    pallas_call x1, Pallas kernels, chain(): pl.pallas_call(kernel, out_shape=jax.ShapeDtypeStruct((rows, dofs), F32),...  88.7 us
    reshape x1, local copies, waits for them, and re-layouts, local(): return out.reshape(storeys, columns, dofs).transpose(2, 0, 1)  2.09 us

profile of v6, /device:TPU:1, one launch (start us, length us, event | category | flops | bytes accessed | tf_op | source)
XLA Modules:
  0.0 90.8 jit_solution(2323246416413858810)
XLA Ops:
  0.0 88.7 %chain.1 = f32[256,768]{1,0:T(8,128)} custom-call(bf16[768,2,128]{2,1,0:T(2,128)(2,1)} %directions_hbm.1, f32[2,768]{1,0:T(2,128)} %pivot_hbm.1, f32[2,768]{1,0:T(2,128)} %transfer_hbm.1, f32[2,768]{1,0:T(2,128)} %disp_hbm.1, s32[2,2,512]{2,1,0:T(2,128)} %bitcast.4, f32[2,512]{1,0:T(2,128)} %weights_hbm.1, bf16[3072,768]{1,0:T(8,128)(2,1)} %analysis_hbm.1, ...), custom_call_target="tpu_custom_call" | custom-call | flops 4831838208 | bytes 9437184 | tf_op jit(solution)/shard_map/chain/pallas_call | solution.py:441
  88.7 2.1 %copy.9 = f32[2,128,768]{1,0,2:T(2,128)} copy(f32[2,128,768]{2,1,0:T(8,128)} %bitcast.3) | data formatting | bytes 1572864 | tf_op jit(solution)/shard_map/reshape | solution.py:461

commit v7 on v6

--- a/solution.py
+++ b/solution.py
@@ -18,14 +18,14 @@
 NT = (((1,), (1,)), ((), ()))
 
 ORDER = (
-    "BAR", "COEF1", "P000", "OPP000", "P012", "Z0", "P003", "OPP001", "P010", "OPP011", "OPP010", "P001", "P002",
-    "RATE1", "Z1", "P013", "P011", "INC", "COEF2", "Z2", "MID000", "MID001", "Z3", "RATE2", "MID011", "MID010",
-    "END000", "END001", "RATE3", "END010", "SC200", "END011", "AG200", "SC201", "AG201", "CAR00", "CAR01", "FL80",
-    "EXP00", "EXQ001", "EXQ002", "EXQ000", "SEN10", "EXP01", "EXQ011", "EXQ010", "EXQ012", "SEN11", "SEN20",
+    "BAR", "P000", "OPP000", "P012", "Z0", "P003", "OPP001", "P010", "OPP011", "OPP010", "P001", "P002", "RATE1",
+    "Z1", "P013", "P011", "INC", "Z2", "MID000", "MID001", "Z3", "RATE2", "MID011", "MID010", "COEF1", "END000",
+    "END001", "RATE3", "END010", "SC200", "END011", "AG200", "SC201", "AG201", "CAR00", "CAR01", "COEF2", "FL80",
+    "EXQ002", "EXQ001", "EXQ000", "EXP00", "SEN10", "EXQ012", "EXQ011", "EXQ010", "EXP01", "SEN11", "SEN20",
     "SEN21", "FL12", "ADJ0", "P100", "OPP100", "P101", "P102", "P103", "OPP101", "ADJ1", "P110", "OPP110", "P113",
     "P112", "MID100", "OPP111", "P111", "MID101", "MID110", "END100", "MID111", "FL24", "END101", "SC210", "END110",
-    "END111", "AG210", "FL40", "SC211", "CAR10", "AG211", "CAR11", "FL66", "EXP10", "EXQ102", "EXQ100", "EXQ101",
-    "OUT0", "FL31", "EXP11", "EXQ111", "EXQ112", "EXQ110", "OUT1",
+    "END111", "AG210", "FL40", "SC211", "CAR10", "AG211", "CAR11", "FL66", "EXQ102", "EXQ101", "EXQ100", "EXP10",
+    "OUT0", "FL31", "EXQ112", "EXQ111", "EXQ110", "EXP11", "OUT1",
 )
 
 
@@ -35,12 +35,12 @@
 
 def kernel(
     directions_hbm, pivot_hbm, transfer_hbm, disp_hbm, pairs_hbm, weights_hbm, analysis_hbm, synthesis_hbm,
-    out_ref,
+    out_hbm,
     directions_ref, pivot_ref, transfer_ref, disp_ref, pairs_ref, weights_ref, load_ref,
-    A, S, E, acc, part, keep, opp_out, opp_in, mid_out, mid_in, early, early_in, late_in,
+    result, A, S, E, acc, part, keep, opp_out, opp_in, mid_out, mid_in, early, early_in, late_in,
     shift, group_in, base, base_in, zone_in, reply, coef, rate_group, rate_zone,
     read_out, read_in, wread, adj,
-    z_sem, in_sem, a_sem, s_sem, x_send, x_recv, k_send, k_recv, l_send, l_recv, a_recv,
+    o_sem, z_sem, in_sem, a_sem, s_sem, x_send, x_recv, k_send, k_recv, l_send, l_recv, a_recv,
     c_send, c_recv, r_send, r_recv, q_send, q_recv,
 ):
     storey = lax.axis_index("storey")
@@ -55,6 +55,7 @@
     hm = dofs // 2
     right, left, oppo = lax.rem(x + 1, NX), lax.rem(x + 3, NX), lax.rem(x + 2, NX)
     pending = []
+    results = []
 
     def xdev(i):
         return (storey, i)
@@ -307,6 +308,8 @@
         late_in[v, k, x, w] = reply[v, k, w]
 
     def expand(v, k, n):
+        if s_copies:
+            s_copies.pop().wait()
         t = (left, right, oppo, x)[n]
         if n == 3:
             for i in wpeers:
@@ -329,11 +332,9 @@
             high = (last.astype(F32) * coef[t, 3:4, :]).astype(BF16)
             val = jnp.concatenate([low, high], axis=0)
             new = mm(val, A[block(t), :], NN)
-        acc[k] = new if n == 3 else acc[k] + new
+        acc[k] = new if n == 2 else acc[k] + new
 
     def expand_own(v, k):
-        if s_copies:
-            s_copies.pop().wait()
         expand(v, k, 3)
 
     quarter = 2 * hc // NX
@@ -366,8 +367,9 @@
 
     def finish(k):
         for s in range(2):
-            at = s * cols + k * hc
-            out_ref[at : at + hc] = -disp_ref[s : s + 1, :] * acc[k, s * hc : (s + 1) * hc]
+            at = pl.ds(s * cols + k * hc, hc)
+            result[at] = -disp_ref[s : s + 1, :] * acc[k, s * hc : (s + 1) * hc]
+            results.append(fetch(result.at[at], out_hbm.at[at], o_sem.at[k, s]))
 
     steps = {
         "INC": build_incidence, "BAR": entered, "Z": along, "COEF1": coefficients_first, "COEF2": coefficients_second,
@@ -386,6 +388,8 @@
         stem = name[:1] if name[0] in "PZ" else name[:4] if name[:3] == "SEN" else name[:3]
         steps[stem](*(int(d) for d in name[len(stem) :]))
     flush(0)
+    for c in results:
+        c.wait()
 
 
 def chain(directions, pivot, transfer, disp, pairs, weights, analysis, synthesis):
@@ -401,6 +405,7 @@
     small = (directions, pivot, transfer, disp, pairs, weights)
     scratch = [vm(a.shape, a.dtype) for a in small] + [
         vm((rows, dofs), BF16),
+        vm((rows, dofs), F32),
         vm((modes, dofs), BF16),
         vm((dofs, modes), BF16),
         vm((2, dofs, sensors), BF16),
@@ -427,7 +432,7 @@
         vm((NU, NX, 2 * hc // NX, sensors), BF16),
         vm((NU, NX, 2 * hc // NX, sensors), BF16),
         vm((NU, 2 * hc, dofs), BF16),
-        pltpu.SemaphoreType.REGULAR((3, 2)),
+        dma((NU, 2)), pltpu.SemaphoreType.REGULAR((3, 2)),
         dma((6,)), dma((4,)), dma((1,)),
         dma((2, NU, 2, 6)), dma((2, NU, 2, 6)),
         dma((NX,)), dma((NX,)),
@@ -436,13 +441,12 @@
         dma((2, 8)), dma((2, 8)),
         dma((NU, 2, 4)), dma((NU, 2, 4)),
     ]
-    in_vmem = pl.BlockSpec(memory_space=pltpu.VMEM)
     in_hbm = pl.BlockSpec(memory_space=pl.ANY)
     return pl.pallas_call(
         kernel,
         out_shape=jax.ShapeDtypeStruct((rows, dofs), F32),
         in_specs=[in_hbm] * 8,
-        out_specs=in_vmem,
+        out_specs=in_hbm,
         scratch_shapes=scratch,
         compiler_params=pltpu.CompilerParams(
             collective_id=0, has_side_effects=True, vmem_limit_bytes=56 * 1024 * 1024

time: 90.9 us -> 90.6 us (level)
  no operation moved by 1% of the time
where the time goes in v7:
time: 90.6 us; the launch traced here: 90.5 us
  Pallas kernels  88.4 us (98%)
  local copies, waits for them, and re-layouts  2.09 us (2%)
    pallas_call x1, Pallas kernels, chain(): pl.pallas_call(kernel, out_shape=jax.ShapeDtypeStruct((rows, dofs), F32),...  88.4 us
    reshape x1, local copies, waits for them, and re-layouts, local(): return out.reshape(storeys, columns, dofs).transpose(2, 0, 1)  2.09 us

profile of v7, /device:TPU:1, one launch (start us, length us, event | category | flops | bytes accessed | tf_op | source)
XLA Modules:
  0.0 90.5 jit_solution(13698080443379990128)
XLA Ops:
  0.0 88.4 %chain.1 = f32[256,768]{1,0:T(8,128)} custom-call(bf16[768,2,128]{2,1,0:T(2,128)(2,1)} %directions_hbm.1, f32[2,768]{1,0:T(2,128)} %pivot_hbm.1, f32[2,768]{1,0:T(2,128)} %transfer_hbm.1, f32[2,768]{1,0:T(2,128)} %disp_hbm.1, s32[2,2,512]{2,1,0:T(2,128)} %bitcast.4, f32[2,512]{1,0:T(2,128)} %weights_hbm.1, bf16[3072,768]{1,0:T(8,128)(2,1)} %analysis_hbm.1, ...), custom_call_target="tpu_custom_call" | custom-call | flops 4831838208 | bytes 9437184 | tf_op jit(solution)/shard_map/chain/pallas_call | solution.py:445
  88.4 2.1 %copy.9 = f32[2,128,768]{1,0,2:T(2,128)} copy(f32[2,128,768]{2,1,0:T(8,128)} %bitcast.3) | data formatting | bytes 1572864 | tf_op jit(solution)/shard_map/reshape | solution.py:465
